TPU v7x, 256 devices: a whole 4x4x8 slice. The times are simulated.
256 devices in a mesh: gy: 64 (over y, z_lo, x, core), gz: 4 (over z_hi).
Axes of the slice: x: 4, y: 4, z: 8 (z_hi: 4, z_lo: 2; z = z_hi * 2 + z_lo), core: 2. Of those that a mesh axis runs over, the one named last changes fastest.
Arguments:
- density: float32 [256, 1024, 1024], P(None, 'gy', 'gz'), may hold values from -16 to 16
Outputs:
- side_view: float32 [3, 256, 1024], P(None, 'gy', 'gz')
- top_view: float32 [3, 256, 1024], P(None, 'gz', 'gy')
All inputs are finite; a program needn't handle non-finite values.
Results may differ from a plain program's by a relative error of at most 0.0003.
Values sent between devices are 32-bit elements; how exact they have to be, the bound alone decides.
A program may use at most 64 MiB of HBM per device.

v0:
```python
import math

import jax
import jax.numpy as jnp
from jax import lax
from jax.sharding import PartitionSpec as P


def padded_2(cells, sides, width):
    for axis, dim in sides:
        count = lax.axis_size(axis)
        ends = count - 1
        head = lax.slice_in_dim(cells, 0, width, axis=dim)
        tail = lax.slice_in_dim(cells, cells.shape[dim] - width, cells.shape[dim], axis=dim)
        cells = jnp.concatenate(
            [
                lax.ppermute(tail, axis, [(i, (i + 1) % count) for i in range(ends)]),
                cells,
                lax.ppermute(head, axis, [((i + 1) % count, i) for i in range(ends)]),
            ],
            axis=dim,
        )
    return cells


def body(density):
    y_factor = 1.0 / math.sqrt(density.shape[1] * lax.axis_size("gy"))
    z_factor = 1.0 / math.sqrt(density.shape[2] * lax.axis_size("gz"))
    padded = padded_2(density, (("gy", 1), ("gz", 2)), 1)
    center = padded[:, 1:-1, 1:-1]
    x_lower = jnp.pad(center[:-1], ((1, 0), (0, 0), (0, 0)))
    x_upper = jnp.pad(center[1:], ((0, 1), (0, 0), (0, 0)))
    y_high = padded[:, 2:, 1:-1]
    y_low = padded[:, :-2, 1:-1]
    z_high = padded[:, 1:-1, 2:]
    z_low = padded[:, 1:-1, :-2]
    grad_x = (x_upper - x_lower) * 0.5
    grad_y = (y_high - y_low) * 0.5
    grad_z = (z_high - z_low) * 0.5
    curve_x = x_upper + x_lower - 2.0 * center
    curve_y = y_high + y_low - 2.0 * center
    curve_z = z_high + z_low - 2.0 * center
    side_part = jnp.stack([grad_z.sum(1), grad_x.sum(1), (curve_x + curve_z).sum(1)])
    top_part = jnp.stack([grad_y.sum(2), grad_x.sum(2), (curve_x + curve_y).sum(2)])
    side_view = lax.psum_scatter(side_part, "gy", scatter_dimension=1, tiled=True) * y_factor
    top_view = lax.psum_scatter(top_part, "gz", scatter_dimension=1, tiled=True) * z_factor
    return (side_view, top_view)


def solution(mesh):
    placed = (P(None, "gy", "gz"),)
    return jax.shard_map(
        body,
        mesh=mesh,
        in_specs=placed,
        out_specs=(P(None, "gy", "gz"), P(None, "gz", "gy")),
        check_vma=False,
    )
```

profile of v0, /device:TPU:1, one launch (start us, length us, event | category | flops | bytes accessed | tf_op | source)
XLA Modules:
  0.0 593.8 jit_solution(6330376666426892756)
XLA Ops:
  8.0 0.0 reduce-scatter.5.cloned.1.call-start
  8.0 2.6 fusion.3
  10.7 4.5 collective-permute-start
  15.2 1.9 collective-permute-start.1
  17.2 5.6 copy.22
  22.8 0.0 collective-permute-done
  22.8 0.2 copy.21
  22.9 0.0 collective-permute-done.1
  22.9 0.2 copy.23
  23.1 0.0 copy-start
  23.1 0.9 pad_maximum_fusion.12
  24.0 1.4 collective-permute-start.2
  25.5 5.5 collective-permute-start.3
  31.0 0.0 copy-done
  31.0 1.5 fusion.2
  32.4 0.0 collective-permute-done.2
  32.4 0.0 collective-permute-done.3
  32.5 6.4 %add_reduce_fusion = (f32[256,16]{0,1:T(8,128)S(1)}, f32[256,256]{0,1:T(8,128)S(1)}, f32[256,16]{0,1:T(8,128)S(1)}, f32[256,256]{0,1:T(8,128)S(1)}) fusion(f32[256,16,256]{0,1,2:T(8,128)S(1)} %copy-done, f32[256,1,256]{0,1,2:T(1,128)S(1)} %copy.23, f32[256,1,256]{0,1,2:T(1,128)S(1)} %copy.21, f32[255,16,256]{0,1,2:T(8,128)S(1)} %get-tuple-element.11, ...), kind=kLoop, calls=%fused_computation.8 | loop fusion | flops 23977984 | bytes 13668352 | tf_op jit(solution)/shard_map/reduce_sum | solution.py:44
  38.9 0.1 copy.43
  39.0 0.1 copy.36
  39.1 0.1 copy.44
  39.2 0.1 copy.37
  39.2 0.0 copy-start.1
  39.2 7.8 %multiply_reduce_fusion = (f32[256,16]{0,1:T(8,128)S(1)}, f32[256,256]{0,1:T(8,128)S(1)}) fusion(f32[256,1,256]{0,1,2:T(1,128)S(1)} %copy.23, f32[256,16,256]{0,1,2:T(8,128)} %copy.22, f32[256,1,256]{0,1,2:T(1,128)S(1)} %copy.21, f32[256,18,1]{0,1,2:T(8,128)S(1)} %collective-permute-done.3, f32[256,18,1]{0,1,2:T(8,128)S(1)} %collective-permute-done.2), kind=kLoop, calls=%fused_computation.9 | loop fusion | flops 14610432 | bytes 5033984 | tf_op jit(solution)/shard_map/reduce_sum | solution.py:44
  47.1 0.1 copy.42
  47.2 0.1 copy.35
  47.3 0.2 copy.40
  47.5 0.9 reshape.6
  48.4 0.0 reduce-scatter.5.cloned.1.call-update
  48.4 0.0 all-reduce.5.cloned.1.call-start
  48.5 0.1 pad_maximum_fusion.8
  48.5 1.2 copy.27
  49.7 0.0 all-reduce.5.cloned.1.call-update
  49.7 0.0 copy-done.1
  49.7 0.6 dynamic-slice
  51.0 26.1 %reduce-scatter.5.cloned.1.call-done = f32[64,48]{1,0:T(8,128)} async-done(((f32[256,48]{1,0:T(8,128)}), f32[64,48]{1,0:T(8,128)}) %reduce-scatter.5.cloned.1.call-update) | async-done | bytes 12304
  77.0 0.9 reshape.7
  77.9 0.1 copy.41
  78.0 0.6 broadcast_multiply_fusion
  78.6 506.4 %all-reduce.5.cloned.1.call-done = f32[3,256,256]{2,1,0:T(8,128)} async-done(((f32[3,256,256]{2,1,0:T(8,128)}), f32[3,256,256]{2,1,0:T(8,128)}) %all-reduce.5.cloned.1.call-update) | async-done | bytes 786448
  585.0 1.3 dynamic-slice_multiply_fusion
  (3 shorter events, 0.0 us)
Async XLA Ops:
  8.0 69.0 %reduce-scatter.5.cloned.1.call-start = ((), (), s32[]{:S(2)}) async-start(), calls=%async_computation.1 | async-start | bytes 163840
  10.7 12.1 %collective-permute-start = (f32[256,1,256]{2,0,1:T(8,128)S(1)}, f32[256,1,256]{2,0,1:T(8,128)S(1)}, u32[]{:S(2)}, u32[]{:S(2)}) collective-permute-start(f32[256,1,256]{2,0,1:T(8,128)S(1)} %copy.45), channel_id=1, source_target_pairs={{0,4},{4,8},{8,12},{12,16},{16,20},{20,24},{24,28},{28,32},{32,36}... | collective-permute-start | bytes 786440 | tf_op jit(solution)/shard_map/ppermute | solution.py:17
  15.2 7.7 %collective-permute-start.1 = (f32[256,1,256]{2,0,1:T(8,128)S(1)}, f32[256,1,256]{2,0,1:T(8,128)S(1)}, u32[]{:S(2)}, u32[]{:S(2)}) collective-permute-start(f32[256,1,256]{2,0,1:T(8,128)S(1)} %copy.46), channel_id=1, source_target_pairs={{4,0},{8,4},{12,8},{16,12},{20,16},{24,20},{28,24},{32,28},{36,32}... | collective-permute-start | bytes 786440 | tf_op jit(solution)/shard_map/ppermute | solution.py:19
  23.1 7.9 %copy-start = (f32[256,16,256]{0,1,2:T(8,128)S(1)}, f32[256,16,256]{0,1,2:T(8,128)}, u32[]{:S(2)}) copy-start(f32[256,16,256]{0,1,2:T(8,128)} %copy.22) | copy-start | bytes 12582916
  24.0 8.4 %collective-permute-start.2 = (f32[256,18,1]{0,1,2:T(8,128)S(1)}, f32[256,18,1]{0,1,2:T(8,128)S(1)}, u32[]{:S(2)}, u32[]{:S(2)}) collective-permute-start(f32[256,18,1]{0,1,2:T(8,128)S(1)} %get-tuple-element.8), channel_id=1, source_target_pairs={{1,0},{2,1},{3,2},{5,4},{6,5},{7,6},{9,8},{10,9},{11,10},{13,12},{... | collective-permute-start | bytes 55304 | tf_op jit(solution)/shard_map/ppermute | solution.py:19
  25.5 7.0 %collective-permute-start.3 = (f32[256,18,1]{0,1,2:T(8,128)S(1)}, f32[256,18,1]{0,1,2:T(8,128)S(1)}, u32[]{:S(2)}, u32[]{:S(2)}) collective-permute-start(f32[256,18,1]{0,1,2:T(8,128)S(1)} %get-tuple-element.9), channel_id=1, source_target_pairs={{0,1},{1,2},{2,3},{4,5},{5,6},{6,7},{8,9},{9,10},{10,11},{12,13},{... | collective-permute-start | bytes 55304 | tf_op jit(solution)/shard_map/ppermute | solution.py:17
  39.2 10.5 %copy-start.1 = (u32[256]{0:T(256)S(1)}, u32[256]{0:T(256)}, u32[]{:S(2)}) copy-start(u32[256]{0:T(256)} %constant.18) | copy-start | bytes 3076
  48.4 536.6 %all-reduce.5.cloned.1.call-start = ((), (), s32[]{:S(2)}) async-start(), calls=%async_computation.2 | async-start | bytes 1572864
Sparse Core Ops, SparseCore 0:
  48.5 28.4 reduce-scatter.4
Sparse Core Ops, SparseCore 1:
  51.5 533.4 all-reduce.4
where the time goes:
time: 595 us; the launch traced here: 594 us
  waiting for transfers between devices  532 us (89%)
  other arithmetic  17.2 us (3%)
  between operations  16.3 us (3%)
  local copies, waits for them, and re-layouts  14.3 us (2%)
  starting transfers between devices  13.5 us (2%)
    unnamed x4, waiting for transfers between devices  532 us
  transfers between devices with their start and end apart: 6, of which 2 were waited for; matrix products, arithmetic and copies ran while one was open for 2% of the time, Pallas kernels for 0%

commit v1 on v0

v1 whole, which is shorter than its diff:
```python
import functools
import math

import jax
import jax.numpy as jnp
from jax import lax
from jax.experimental import pallas as pl
from jax.experimental.pallas import tpu as pltpu
from jax.sharding import PartitionSpec as P

MESH = pl.DeviceIdType.MESH
CHUNKS = 4
ORDER = (2, 1, 3, 0)


def iota(axis):
    return lax.broadcasted_iota(jnp.int32, (8, 128), axis)


def side_maps(total, low_x, high_x, low_z, high_z, factor):
    row, lane = iota(0), iota(1)
    lower_x = jnp.where(row % 4 == 0, pltpu.roll(low_x, 5, 0), pltpu.roll(total, 1, 0))
    upper_x = jnp.where(row % 4 == 3, pltpu.roll(high_x, 3, 0), pltpu.roll(total, 7, 0))
    down = pltpu.roll(total, 1, 1)
    up = pltpu.roll(total, 127, 1)
    low_edge = pltpu.roll(jnp.where(row >= 4, low_z, total), 4, 0)
    high_edge = pltpu.roll(jnp.where(row < 4, high_z, total), 4, 0)
    lower_z = jnp.where(lane == 0, pltpu.roll(low_edge, 1, 1), down)
    upper_z = jnp.where(lane == 127, pltpu.roll(high_edge, 127, 1), up)
    grad_z = (upper_z - lower_z) * (0.5 * factor)
    grad_x = (upper_x - lower_x) * (0.5 * factor)
    curve = (upper_x + lower_x + upper_z + lower_z - 4.0 * total) * factor
    return grad_z, grad_x, curve


def top_maps(total, low_y, high_y, low_x, high_x, factor):
    row, lane = iota(0), iota(1)
    lower_x = jnp.where(lane % 64 == 0, pltpu.roll(low_x, 65, 1), pltpu.roll(total, 1, 1))
    upper_x = jnp.where(lane % 64 == 63, pltpu.roll(high_x, 63, 1), pltpu.roll(total, 127, 1))
    low_edge = pltpu.roll(jnp.where(lane >= 64, low_y, total), 64, 1)
    high_edge = pltpu.roll(jnp.where(lane < 64, high_y, total), 64, 1)
    lower_y = pltpu.roll(jnp.where(row == 7, low_edge, total), 1, 0)
    upper_y = pltpu.roll(jnp.where(row == 0, high_edge, total), 7, 0)
    grad_y = (upper_y - lower_y) * (0.5 * factor)
    grad_x = (upper_x - lower_x) * (0.5 * factor)
    curve = (upper_x + lower_x + upper_y + lower_y - 4.0 * total) * factor
    return grad_y, grad_x, curve


def kernel(ny, nz, y_factor, z_factor, density, side_out, top_out, cells, side_part, side_recv, side_halo, top_part,
           top_recv, top_halo, load_sem, send_sem, recv_sem):
    rows, depth, width = cells.shape
    span = ny // CHUNKS
    chunk_rows = rows // CHUNKS
    me_y, me_z = lax.axis_index("gy"), lax.axis_index("gz")
    order = [lax.rem(me_y // span + step, CHUNKS) for step in ORDER]
    loads = []
    for step, chunk in enumerate(order):
        at = pl.ds(chunk * chunk_rows, chunk_rows)
        loads.append(pltpu.make_async_copy(density.at[at], cells.at[at], load_sem.at[step]))
        loads[-1].start()

    barrier = pltpu.get_barrier_semaphore()

    def greet_y(step, carry):
        pl.semaphore_signal(barrier, inc=1, device_id=(lax.rem(me_y + step, ny), me_z), device_id_type=MESH)
        return carry

    def greet_z(step, carry):
        pl.semaphore_signal(barrier, inc=1, device_id=(me_y, lax.rem(me_z + step, nz)), device_id_type=MESH)
        return carry

    lax.fori_loop(1, ny, greet_y, 0)
    lax.fori_loop(1, nz, greet_z, 0)

    groups = chunk_rows // 8
    for step, chunk in enumerate(order):
        loads[step].wait()

        def add_rows(group, carry):
            group = chunk * groups + group
            added = cells[pl.ds(group * 8, 8)].sum(axis=1)
            first, last = added[:, :128], added[:, 128:]
            side_part[2 * group] = jnp.concatenate([first[:4], last[:4]], axis=0)
            side_part[2 * group + 1] = jnp.concatenate([first[4:], last[4:]], axis=0)
            return carry

        lax.fori_loop(0, groups, add_rows, 0, unroll=True)
        if step == 0:
            pl.semaphore_wait(barrier, ny - 1 + nz - 1)

        def send(turn, carry):
            to = chunk * span + lax.rem(me_y + turn, span)

            @pl.when(to != me_y)
            def _():
                pltpu.make_async_remote_copy(
                    src_ref=side_part.at[to],
                    dst_ref=side_recv.at[me_y],
                    send_sem=send_sem.at[0],
                    recv_sem=recv_sem.at[0],
                    device_id=(to, me_z),
                    device_id_type=MESH,
                ).start()

            return carry

        lax.fori_loop(0, span, send, 0)

    side_recv[me_y] = side_part[me_y]

    ones = jnp.ones((width, 128), jnp.bfloat16)
    lane = iota(1)

    def add_columns(owner, carry):
        block = jnp.zeros((8, 128), jnp.float32)
        for k in range(8):
            piece = cells[pl.ds(owner * 64 + 8 * k, 8)].reshape(8 * depth, width)
            high = piece.astype(jnp.bfloat16)
            low = (piece - high.astype(jnp.float32)).astype(jnp.bfloat16)
            added = jnp.dot(high, ones, preferred_element_type=jnp.float32)
            added += jnp.dot(low, ones, preferred_element_type=jnp.float32)
            for x in range(8):
                for half in range(2):
                    at = 16 * x + 8 * half
                    block = jnp.where(lane == 64 * half + 8 * k + x, added[at : at + 8], block)
        top_part[owner] = block
        return carry

    lax.fori_loop(0, nz, add_columns, 0)

    for turn in range(1, nz):
        to = lax.rem(me_z + turn, nz)
        pltpu.make_async_remote_copy(
            src_ref=top_part.at[to],
            dst_ref=top_recv.at[me_z],
            send_sem=send_sem.at[1],
            recv_sem=recv_sem.at[1],
            device_id=(me_y, to),
            device_id_type=MESH,
        ).start()
    top_recv[me_z] = top_part[me_z]

    def wait_all(ref, count, sem):
        held = ref.at[pl.ds(0, count)]
        pltpu.make_async_copy(held, held, sem).wait()

    next_y, last_y = lax.rem(me_y + 1, ny), lax.rem(me_y + ny - 1, ny)
    next_z, last_z = lax.rem(me_z + 1, nz), lax.rem(me_z + nz - 1, nz)
    peers = ((next_y, me_z), (last_y, me_z), (me_y, next_z), (me_y, last_z))

    def send_halo(source, halo, at):
        for slot, peer in enumerate(peers):
            pltpu.make_async_remote_copy(
                src_ref=source,
                dst_ref=halo.at[slot],
                send_sem=send_sem.at[at],
                recv_sem=recv_sem.at[at],
                device_id=peer,
                device_id_type=MESH,
            ).start()

    def edged(halo, slot, there):
        return jnp.where(there, halo[slot], 0.0)

    wait_all(side_recv, ny - 1, recv_sem.at[0])
    side_total = side_recv[...].sum(axis=0)
    wait_all(side_part, ny - 1, send_sem.at[0])
    side_part[0] = side_total
    send_halo(side_part.at[0], side_halo, 2)

    wait_all(top_recv, nz - 1, recv_sem.at[1])
    top_total = top_recv[...].sum(axis=0)
    wait_all(top_part, nz - 1, send_sem.at[1])
    top_part[0] = top_total
    send_halo(top_part.at[0], top_halo, 3)

    wait_all(side_halo, 4, recv_sem.at[2])
    maps = side_maps(
        side_total,
        edged(side_halo, 0, me_y > 0),
        edged(side_halo, 1, me_y < ny - 1),
        edged(side_halo, 2, me_z > 0),
        edged(side_halo, 3, me_z < nz - 1),
        y_factor,
    )
    for i, found in enumerate(maps):
        side_out[i, :, 0:128] = found[:4]
        side_out[i, :, 128:256] = found[4:]

    wait_all(top_halo, 4, recv_sem.at[3])
    maps = top_maps(
        top_total,
        edged(top_halo, 0, me_y > 0),
        edged(top_halo, 1, me_y < ny - 1),
        edged(top_halo, 2, me_z > 0),
        edged(top_halo, 3, me_z < nz - 1),
        z_factor,
    )
    for i, found in enumerate(maps):
        top_out[i, 0:8, :] = found[:, :64]
        top_out[i, 8:16, :] = found[:, 64:]

    wait_all(side_halo, 4, send_sem.at[2])
    wait_all(top_halo, 4, send_sem.at[3])


def solution(mesh):
    ny, nz = mesh.shape["gy"], mesh.shape["gz"]

    def body(density):
        rows, depth, width = density.shape
        call = pl.pallas_call(
            functools.partial(kernel, ny, nz, 1.0 / math.sqrt(depth * ny), 1.0 / math.sqrt(width * nz)),
            out_shape=(
                jax.ShapeDtypeStruct((3, rows // ny, width), jnp.float32),
                jax.ShapeDtypeStruct((3, depth, rows // nz), jnp.float32),
            ),
            in_specs=[pl.BlockSpec(memory_space=pl.ANY)],
            out_specs=(pl.BlockSpec(memory_space=pltpu.VMEM), pl.BlockSpec(memory_space=pltpu.VMEM)),
            scratch_shapes=[
                pltpu.VMEM((rows, depth, width), jnp.float32),
                pltpu.VMEM((ny, 8, 128), jnp.float32),
                pltpu.VMEM((ny, 8, 128), jnp.float32),
                pltpu.VMEM((4, 8, 128), jnp.float32),
                pltpu.VMEM((nz, 8, 128), jnp.float32),
                pltpu.VMEM((nz, 8, 128), jnp.float32),
                pltpu.VMEM((4, 8, 128), jnp.float32),
                pltpu.SemaphoreType.DMA((CHUNKS,)),
                pltpu.SemaphoreType.DMA((4,)),
                pltpu.SemaphoreType.DMA((4,)),
            ],
            compiler_params=pltpu.CompilerParams(
                collective_id=0, has_side_effects=True, vmem_limit_bytes=56 * 1024 * 1024
            ),
        )
        side, top = call(density)
        return side, jnp.swapaxes(top, 1, 2)

    return jax.shard_map(
        body,
        mesh=mesh,
        in_specs=(P(None, "gy", "gz"),),
        out_specs=(P(None, "gy", "gz"), P(None, "gz", "gy")),
        check_vma=False,
    )
```

time: 595 us -> 26 us (0.04)
  waiting for transfers between devices: 532 us -> 0 us
  Pallas kernels: 0 us -> 22.5 us
  other arithmetic: 17.2 us -> 0 us
  between operations: 16.3 us -> 0.64 us
  starting transfers between devices: 13.5 us -> 0 us
  local copies, waits for them, and re-layouts: 14.3 us -> 2.65 us
    unnamed x4 -> x0, waiting for transfers between devices: 532 us -> none
    pallas_call x0 -> x1, Pallas kernels: none -> 22.5 us  [body(): side, top = call(density)]
    reduce_sum x2 -> x0, other arithmetic: 14.3 us -> none  [the longest x1 7.84 us: body(): grad_y.sum(2)]
    ppermute x4 -> x0, starting transfers between devices: 13.4 us -> none  [the longest x2 10 us: padded_2(): lax.ppermute(tail, axis, [(i, (i + 1) % count) for i in range(ends)])]
  transfers between devices with their start and end apart: 6 -> 0, of which waited for: 2 -> 0; matrix products, arithmetic and copies ran while one was open for 2% -> 0% of each run, Pallas kernels for 0% -> 0%
where the time goes in v1:
time: 26 us; the launch traced here: 25.8 us
  Pallas kernels  22.5 us (87%)
  local copies, waits for them, and re-layouts  2.65 us (10%)
  between operations  0.64 us (2%)
    pallas_call x1, Pallas kernels, body(): side, top = call(density)  22.5 us
    unnamed x2, local copies, waits for them, and re-layouts  2.65 us

profile of v1, /device:TPU:1, one launch (start us, length us, event | category | flops | bytes accessed | tf_op | source)
XLA Modules:
  0.0 25.8 jit_solution(15290325759767213311)
XLA Ops:
  0.6 22.5 %shard_map.30 = (f32[3,4,256]{2,1,0:T(4,128)}, f32[3,16,64]{2,1,0:T(8,128)}) custom-call(f32[256,16,256]{2,1,0:T(8,128)} %density.1), custom_call_target="tpu_custom_call" | custom-call | tf_op jit(solution)/shard_map/pallas_call | solution.py:237
  23.1 1.3 %copy.5 = f32[3,4,256]{2,1,0:T(4,128)} copy(f32[3,4,256]{2,1,0:T(4,128)} %get-tuple-element.8) | data formatting | bytes 24576
  24.4 1.3 %copy.6 = f32[3,64,16]{1,2,0:T(8,128)} copy(f32[3,64,16]{1,2,0:T(8,128)} %bitcast.1) | data formatting | bytes 24576

commit v2 on v0

v2 whole, which is shorter than its diff:
```python
import functools
import math

import jax
import jax.numpy as jnp
from jax import lax
from jax.experimental import pallas as pl
from jax.experimental.pallas import tpu as pltpu
from jax.sharding import PartitionSpec as P

MESH = pl.DeviceIdType.MESH
CHUNKS = 8


def iota(axis):
    return lax.broadcasted_iota(jnp.int32, (8, 128), axis)


def side_maps(total, low_x, high_x, low_z, high_z, factor):
    row, lane = iota(0), iota(1)
    lower_x = jnp.where(row % 4 == 0, pltpu.roll(low_x, 5, 0), pltpu.roll(total, 1, 0))
    upper_x = jnp.where(row % 4 == 3, pltpu.roll(high_x, 3, 0), pltpu.roll(total, 7, 0))
    down = pltpu.roll(total, 1, 1)
    up = pltpu.roll(total, 127, 1)
    low_edge = pltpu.roll(jnp.where(row >= 4, low_z, total), 4, 0)
    high_edge = pltpu.roll(jnp.where(row < 4, high_z, total), 4, 0)
    lower_z = jnp.where(lane == 0, pltpu.roll(low_edge, 1, 1), down)
    upper_z = jnp.where(lane == 127, pltpu.roll(high_edge, 127, 1), up)
    grad_z = (upper_z - lower_z) * (0.5 * factor)
    grad_x = (upper_x - lower_x) * (0.5 * factor)
    curve = (upper_x + lower_x + upper_z + lower_z - 4.0 * total) * factor
    return grad_z, grad_x, curve


def top_maps(total, low_y, high_y, factor):
    row = iota(0)
    first, last = total
    lower_y = [pltpu.roll(jnp.where(row == 7, a, b), 1, 0) for a, b in ((low_y, first), (first, last))]
    upper_y = [pltpu.roll(jnp.where(row == 0, a, b), 7, 0) for a, b in ((last, first), (high_y, last))]
    for here, lower, upper in zip(total, lower_y, upper_y):
        lower_x, upper_x = pltpu.roll(here, 1, 1), pltpu.roll(here, 127, 1)
        yield (
            (upper - lower) * (0.5 * factor),
            (upper_x - lower_x) * (0.5 * factor),
            (upper_x + lower_x + upper + lower - 4.0 * here) * factor,
        )


def kernel(ny, nz, y_factor, z_factor, density, maps_out, cells, side_part, side_recv, side_total, side_halo, top_half,
           top_part, top_recv, top_total, top_halo, load_sem, send_sem, recv_sem, line_sem, side_sem, top_sem):
    rows, depth, width = cells.shape
    span = rows // CHUNKS
    owners = ny // CHUNKS
    me_y, me_z = lax.axis_index("gy"), lax.axis_index("gz")

    def load(j):
        at = pl.ds(j * span, span)
        return pltpu.make_async_copy(density.at[at], cells.at[at], load_sem.at[j])

    for j in range(CHUNKS):
        load(j).start()

    def remote(src, dst, send, recv, peer):
        return pltpu.make_async_remote_copy(
            src_ref=src, dst_ref=dst, send_sem=send, recv_sem=recv, device_id=peer, device_id_type=MESH
        )

    barrier = pltpu.get_barrier_semaphore()
    for to in range(ny):
        @pl.when(me_y != to)
        def _():
            pl.semaphore_signal(barrier, inc=1, device_id=(to, me_z), device_id_type=MESH)

    for z in range(1, nz):
        @pl.when(me_z < z)
        def _():
            pl.semaphore_signal(barrier, inc=1, device_id=(me_y, z), device_id_type=MESH)

    lane = iota(1)

    def add(j, carry):
        load(j).wait()
        block = jnp.zeros((8, 128), jnp.float32)
        place = lane - (j * span) % 64
        for k in range(span // 8):
            piece = cells[pl.ds(j * span + 8 * k, 8)]
            added = piece.sum(axis=1)
            first, last = added[:, :128], added[:, 128:]
            side_part[j * owners + 2 * k] = jnp.concatenate([first[:4], last[:4]], axis=0)
            side_part[j * owners + 2 * k + 1] = jnp.concatenate([first[4:], last[4:]], axis=0)
            added = (piece[:, :, :128] + piece[:, :, 128:]).sum(axis=2, keepdims=True)
            for x in range(8):
                for half in range(2):
                    here = added[x, 8 * half : 8 * half + 8]
                    block = jnp.where(place == 64 * half + 8 * k + x, here, block)
        top_half[j] = block
        return carry

    lax.fori_loop(0, CHUNKS, add, 0)

    pieces = CHUNKS // nz
    packed = []
    for z in range(nz):
        block = top_half[pieces * z]
        for i in range(1, pieces):
            block += top_half[pieces * z + i]
        packed.append(block)
    nothing = jnp.zeros((8, 128), jnp.float32)
    for z in range(nz):
        here = packed[z]
        above = packed[z + 1] if z + 1 < nz else nothing
        below = packed[z - 1] if z else nothing
        around = jnp.where(lane == 64, above, jnp.where(lane == 127, below, 0.0))
        turned = jnp.where(lane == 64, pltpu.roll(above, 64, 1), jnp.where(lane == 127, pltpu.roll(below, 64, 1), 0.0))
        top_part[z, 0] = jnp.where(lane < 64, here, turned)
        top_part[z, 1] = jnp.where(lane < 64, pltpu.roll(here, 64, 1), around)

    def send_top(z):
        remote(top_part.at[z], top_recv.at[me_z], send_sem.at[1], line_sem.at[me_z], (me_y, z)).start()

    def wait_top(z):
        pltpu.make_async_copy(top_recv.at[z], top_recv.at[z], line_sem.at[z]).wait()

    def wait_all(ref, count, sem):
        held = ref.at[pl.ds(0, count)]
        pltpu.make_async_copy(held, held, sem).wait()

    pl.semaphore_wait(barrier, ny - 1 + me_z)
    for z in range(nz - 1):
        @pl.when(me_z > z)
        def _():
            send_top(z)

    for to in range(ny):
        @pl.when(me_y != to)
        def _():
            remote(side_part.at[to], side_recv.at[me_y], send_sem.at[0], recv_sem.at[0], (to, me_z)).start()

    side_recv[me_y] = side_part[me_y]
    top_recv[me_z] = top_part[me_z]

    edges = (
        (me_y < ny - 1, (me_y + 1, me_z), me_y > 0),
        (me_y > 0, (me_y - 1, me_z), me_y < ny - 1),
        (me_z < nz - 1, (me_y, me_z + 1), me_z > 0),
        (me_z > 0, (me_y, me_z - 1), me_z < nz - 1),
    )

    def side_copy(slot):
        return remote(side_total, side_halo.at[slot], side_sem.at[slot], side_sem.at[4 + slot], edges[slot][1])

    def top_copy(slot):
        return remote(top_total.at[1 - slot], top_halo.at[slot], top_sem.at[slot], top_sem.at[2 + slot], edges[slot][1])

    def start(copy, slot):
        pl.when(edges[slot][0])(lambda: copy(slot).start())

    def wait_recv(copy, slot):
        pl.when(edges[slot][2])(lambda: copy(slot).wait_recv())

    def wait_send(copy, slot):
        pl.when(edges[slot][0])(lambda: copy(slot).wait_send())

    for slot, (_, _, receives) in enumerate(edges):
        @pl.when(jnp.logical_not(receives))
        def _():
            side_halo[slot] = nothing
            if slot < 2:
                top_halo[slot] = nothing

    wait_all(side_recv, ny - 1, recv_sem.at[0])
    side_sum = side_recv[...].sum(axis=0)
    side_total[...] = side_sum
    for slot in (3, 0, 1):
        start(side_copy, slot)

    for z in range(1, nz):
        @pl.when(me_z < z)
        def _():
            wait_top(z)
            send_top(z)

        pl.when(me_z + 1 == z)(lambda: side_copy(2).start())

    for z in range(nz - 1):
        @pl.when(me_z > z)
        def _():
            wait_top(z)

    top_sum = top_recv[...].sum(axis=0)
    top_total[...] = top_sum
    for slot in (0, 1):
        start(top_copy, slot)

    for slot in range(4):
        wait_recv(side_copy, slot)
    for i, found in enumerate(side_maps(side_sum, *(side_halo[i] for i in range(4)), y_factor)):
        maps_out[i] = found
    for slot in (0, 1):
        wait_recv(top_copy, slot)
    for half, maps in enumerate(top_maps((top_sum[0], top_sum[1]), top_halo[0], top_halo[1], z_factor)):
        for i, found in enumerate(maps):
            maps_out[3 + 2 * i + half] = found

    wait_all(side_recv, ny - 1, send_sem.at[0])
    wait_all(top_recv, nz - 1, send_sem.at[1])
    for slot in range(4):
        wait_send(side_copy, slot)
    for slot in (0, 1):
        wait_send(top_copy, slot)


def unpack(maps, side_out, top_out):
    for i in range(3):
        side_out[i, :, 0:128] = maps[i, :4]
        side_out[i, :, 128:256] = maps[i, 4:]
        top_out[i, 0:8, :] = maps[3 + 2 * i, :, :64]
        top_out[i, 8:16, :] = maps[4 + 2 * i, :, :64]


def solution(mesh):
    ny, nz = mesh.shape["gy"], mesh.shape["gz"]

    def body(density):
        rows, depth, width = density.shape

        def blocks(*count):
            return pltpu.VMEM((*count, 8, 128), jnp.float32)

        vmem = pl.BlockSpec(memory_space=pltpu.VMEM)
        maps = pl.pallas_call(
            functools.partial(kernel, ny, nz, 1.0 / math.sqrt(depth * ny), 1.0 / math.sqrt(width * nz)),
            out_shape=pltpu.VMEM((9, 8, 128), jnp.float32),
            in_specs=[pl.BlockSpec(memory_space=pltpu.HBM)],
            out_specs=vmem,
            scratch_shapes=[
                pltpu.VMEM((rows, depth, width), jnp.float32),
                blocks(ny),
                blocks(ny),
                blocks(),
                blocks(4),
                blocks(CHUNKS),
                blocks(nz, 2),
                blocks(nz, 2),
                blocks(2),
                blocks(2),
                pltpu.SemaphoreType.DMA((CHUNKS,)),
                pltpu.SemaphoreType.DMA((2,)),
                pltpu.SemaphoreType.DMA((1,)),
                pltpu.SemaphoreType.DMA((nz,)),
                pltpu.SemaphoreType.DMA((8,)),
                pltpu.SemaphoreType.DMA((4,)),
            ],
            compiler_params=pltpu.CompilerParams(
                collective_id=0, has_side_effects=True, vmem_limit_bytes=16 * 1024 * 1024
            ),
            name="views",
        )(pltpu.with_memory_space_constraint(density, pltpu.HBM))
        side, top = pl.pallas_call(
            unpack,
            out_shape=(
                jax.ShapeDtypeStruct((3, rows // ny, width), jnp.float32),
                jax.ShapeDtypeStruct((3, depth, rows // nz), jnp.float32),
            ),
            in_specs=[vmem],
            out_specs=(vmem, vmem),
            name="unpack",
        )(pltpu.with_memory_space_constraint(maps, pltpu.VMEM))
        return side, jnp.swapaxes(top, 1, 2)

    return jax.shard_map(
        body,
        mesh=mesh,
        in_specs=(P(None, "gy", "gz"),),
        out_specs=(P(None, "gy", "gz"), P(None, "gz", "gy")),
        check_vma=False,
    )
```

time: 595 us -> 20.2 us (0.03)
  waiting for transfers between devices: 532 us -> 0 us
  Pallas kernels: 0 us -> 19.3 us
  other arithmetic: 17.2 us -> 0 us
  between operations: 16.3 us -> 0.64 us
  local copies, waits for them, and re-layouts: 14.3 us -> 0 us
  starting transfers between devices: 13.5 us -> 0 us
    unnamed x4 -> x0, waiting for transfers between devices: 532 us -> none
    pallas_call x0 -> x2, Pallas kernels: none -> 19.3 us  [the longest x1 18.7 us: body(): pl.pallas_call(functools.partial(kernel, ny, nz, 1.0 / math.sqrt(depth *...]
    reduce_sum x2 -> x0, other arithmetic: 14.3 us -> none  [the longest x1 7.84 us: body(): grad_y.sum(2)]
    ppermute x4 -> x0, starting transfers between devices: 13.4 us -> none  [the longest x2 10 us: padded_2(): lax.ppermute(tail, axis, [(i, (i + 1) % count) for i in range(ends)])]
    unnamed x15 -> x0, local copies, waits for them, and re-layouts: 8.6 us -> none
  transfers between devices with their start and end apart: 6 -> 0, of which waited for: 2 -> 0; matrix products, arithmetic and copies ran while one was open for 2% -> 0% of each run, Pallas kernels for 0% -> 0%
where the time goes in v2:
time: 20.2 us; the launch traced here: 20 us
  Pallas kernels  19.3 us (96%)
  between operations  0.64 us (3%)
    pallas_call x1, Pallas kernels, body(): pl.pallas_call(functools.partial(kernel, ny, nz, 1.0 / math.sqrt(depth *...  18.7 us
    pallas_call x1, Pallas kernels, body(): pl.pallas_call(unpack, out_shape=(jax.ShapeDtypeStruct((3, rows // ny, wi...  0.62 us

profile of v2, /device:TPU:1, one launch (start us, length us, event | category | flops | bytes accessed | tf_op | source)
XLA Modules:
  0.0 20.0 jit_solution(1004772334620843636)
XLA Ops:
  0.6 18.7 %views.1.maps = f32[9,8,128]{2,1,0:T(8,128)S(1)} custom-call(f32[256,16,256]{2,1,0:T(8,128)} %density.1), custom_call_target="tpu_custom_call" | custom-call | tf_op jit(solution)/shard_map/views/pallas_call | solution.py:231
  19.4 0.6 %unpack.1 = (f32[3,4,256]{2,1,0:T(4,128)}, f32[3,16,64]{2,1,0:T(8,128)}) custom-call(f32[9,8,128]{2,1,0:T(8,128)S(1)} %views.1.maps), custom_call_target="tpu_custom_call" | custom-call | tf_op jit(solution)/shard_map/unpack/pallas_call | solution.py:259

commit v3 on v2

v3 whole, which is shorter than its diff:
```python
import functools
import math

import jax
import jax.numpy as jnp
from jax import lax
from jax.experimental import pallas as pl
from jax.experimental.pallas import tpu as pltpu
from jax.sharding import PartitionSpec as P

MESH = pl.DeviceIdType.MESH
CHUNKS = 8


def iota(axis):
    return lax.broadcasted_iota(jnp.int32, (8, 128), axis)


def stencil(here, lower_a, upper_a, lower_x, upper_x, factor):
    return (
        (upper_a - lower_a) * (0.5 * factor),
        (upper_x - lower_x) * (0.5 * factor),
        (upper_x + lower_x + upper_a + lower_a - 4.0 * here) * factor,
    )


def side_maps(parts, low_x, high_x, low_z, high_z, factor):
    row, lane = iota(0), iota(1)
    around = (low_z, *parts, high_z)
    for h, here in enumerate(parts):
        yield stencil(
            here,
            pltpu.roll(jnp.where(lane == 127, around[h], here), 1, 1),
            pltpu.roll(jnp.where(lane == 0, around[h + 2], here), 127, 1),
            pltpu.roll(jnp.where(row == 7, low_x[h], here), 1, 0),
            pltpu.roll(jnp.where(row == 0, high_x[h], here), 7, 0),
            factor,
        )


def top_maps(parts, low_y, high_y, factor):
    row = iota(0)
    around = (low_y, *parts, high_y)
    for h, here in enumerate(parts):
        yield stencil(
            here,
            pltpu.roll(jnp.where(row == 7, around[h], here), 1, 0),
            pltpu.roll(jnp.where(row == 0, around[h + 2], here), 7, 0),
            pltpu.roll(here, 1, 1),
            pltpu.roll(here, 127, 1),
            factor,
        )


def kernel(ny, nz, y_factor, z_factor, density, maps_out, cells, side_part, side_mate, side_recv, side_total, side_halo,
           top_half, top_part, top_recv, top_total, top_halo, maps_mate, load_sem, mate_sem, side_sem, top_sem, halo_sem,
           maps_sem, ready_sem):
    rows, depth, width = cells.shape
    span = rows // CHUNKS
    chips = ny // 2
    me_y, me_z = lax.axis_index("gy"), lax.axis_index("gz")
    chip, core = me_y // 2, me_y % 2
    leads, follows = core == 1, core == 0
    lead, mate = (2 * chip + 1, me_z), (2 * chip, me_z)

    def load(j):
        at = pl.ds(j * span, span)
        return pltpu.make_async_copy(density.at[at], cells.at[at], load_sem.at[j])

    for j in range(CHUNKS):
        load(j).start()

    def remote(src, dst, send, recv, peer):
        return pltpu.make_async_remote_copy(
            src_ref=src, dst_ref=dst, send_sem=send, recv_sem=recv, device_id=peer, device_id_type=MESH
        )

    def signal(sem, peer):
        pl.semaphore_signal(sem, inc=1, device_id=peer, device_id_type=MESH)

    def wait_all(ref, sem):
        pltpu.make_async_copy(ref, ref, sem).wait()

    barrier = pltpu.get_barrier_semaphore()

    @pl.when(leads)
    def _():
        signal(barrier, mate)
        for n in range(chips):
            pl.when(chip != n)(lambda: signal(barrier, (2 * n + 1, me_z)))
        for z in range(1, nz):
            pl.when(me_z < z)(lambda: signal(barrier, (me_y, z)))

    @pl.when(follows)
    def _():
        pl.semaphore_wait(barrier, 1)

    lane = iota(1)

    def add(j, carry):
        load(j).wait()
        block = jnp.zeros((8, 128), jnp.float32)
        place = lane - (j * span) % 64
        for k in range(span // 8):
            piece = cells[pl.ds(j * span + 8 * k, 8)]
            added = piece.sum(axis=1)
            side_part[j * (span // 8) + k, 0] = added[:, :128]
            side_part[j * (span // 8) + k, 1] = added[:, 128:]
            added = (piece[:, :, :128] + piece[:, :, 128:]).sum(axis=2, keepdims=True)
            for x in range(8):
                for half in range(2):
                    here = added[x, 8 * half : 8 * half + 8]
                    block = jnp.where(place == 64 * half + 8 * k + x, here, block)
        top_half[j] = block

        @pl.when(follows)
        def _():
            at = pl.ds(j * (span // 8), span // 8)
            remote(side_part.at[at], side_mate.at[at], mate_sem.at[0], mate_sem.at[1], lead).start()

        return carry

    lax.fori_loop(0, CHUNKS, add, 0)

    pieces = CHUNKS // nz
    packed = []
    for z in range(nz):
        block = top_half[pieces * z]
        for i in range(1, pieces):
            block += top_half[pieces * z + i]
        packed.append(block)
    nothing = jnp.zeros((8, 128), jnp.float32)
    for z in range(nz):
        here = packed[z]
        above = packed[z + 1] if z + 1 < nz else nothing
        below = packed[z - 1] if z else nothing
        around = jnp.where(lane == 64, above, jnp.where(lane == 127, below, 0.0))
        turned = jnp.where(lane == 64, pltpu.roll(above, 64, 1), jnp.where(lane == 127, pltpu.roll(below, 64, 1), 0.0))
        top_part[core, z, 0] = jnp.where(lane < 64, here, turned)
        top_part[core, z, 1] = jnp.where(lane < 64, pltpu.roll(here, 64, 1), around)

    @pl.when(follows)
    def _():
        remote(top_part.at[0], top_part.at[0], mate_sem.at[2], mate_sem.at[3], lead).start()
        wait_all(side_part, mate_sem.at[0])
        wait_all(top_part.at[0], mate_sem.at[2])
        wait_all(maps_out.at[pl.ds(0, 6)], maps_sem.at[2])
        wait_all(maps_out.at[pl.ds(6, 6)], maps_sem.at[3])

    @pl.when(leads)
    def _():
        edges = (
            (chip < chips - 1, (me_y + 2, me_z), chip > 0),
            (chip > 0, (me_y - 2, me_z), chip < chips - 1),
            (me_z < nz - 1, (me_y, me_z + 1), me_z > 0),
            (me_z > 0, (me_y, me_z - 1), me_z < nz - 1),
        )

        def halo(slot):
            if slot < 2:
                src, dst = side_total, side_halo.at[slot]
            elif slot < 4:
                src, dst = side_total.at[3 - slot], side_halo.at[2, slot - 2]
            else:
                src, dst = top_total.at[3 * (5 - slot)], top_halo.at[slot - 4]
            return remote(src, dst, halo_sem.at[slot], halo_sem.at[6 + slot], edges[slot % 4][1])

        def start(slot):
            pl.when(edges[slot % 4][0])(lambda: halo(slot).start())

        def wait_recv(slot):
            pl.when(edges[slot % 4][2])(lambda: halo(slot).wait_recv())

        def wait_send(slot):
            pl.when(edges[slot % 4][0])(lambda: halo(slot).wait_send())

        def send_top(z):
            for c in range(2):
                remote(top_part.at[c, z], top_recv.at[me_z, c], top_sem.at[0], top_sem.at[1], (me_y, z)).start()

        @pl.when(jnp.logical_not(edges[0][2]))
        def _():
            side_halo[0] = jnp.zeros((2, 8, 128), jnp.float32)
            top_halo[0] = nothing

        @pl.when(jnp.logical_not(edges[1][2]))
        def _():
            side_halo[1] = jnp.zeros((2, 8, 128), jnp.float32)
            top_halo[1] = nothing

        @pl.when(jnp.logical_not(edges[2][2]))
        def _():
            side_halo[2, 0] = nothing

        @pl.when(jnp.logical_not(edges[3][2]))
        def _():
            side_halo[2, 1] = nothing

        pl.semaphore_wait(barrier, chips - 1 + me_z)
        for z in range(nz - 1):
            pl.when(me_z > z)(lambda: signal(ready_sem.at[me_z], (me_y, z)))
        wait_all(top_part.at[0], mate_sem.at[3])
        for z in range(nz - 1):
            pl.when(me_z > z)(lambda: send_top(z))
        wait_all(side_mate, mate_sem.at[1])
        side_part[...] += side_mate[...]
        for n in range(chips):
            @pl.when(chip != n)
            def _():
                remote(side_part.at[n], side_recv.at[chip], side_sem.at[0], side_sem.at[1], (2 * n + 1, me_z)).start()

        side_recv[chip] = side_part[chip]
        top_recv[me_z, 0] = top_part[0, me_z]
        top_recv[me_z, 1] = top_part[1, me_z]

        wait_all(side_recv.at[pl.ds(0, chips - 1)], side_sem.at[1])
        side_total[...] = side_recv[...].sum(axis=0)
        for slot in (3, 0, 1):
            start(slot)
        for z in range(1, nz):
            @pl.when(me_z < z)
            def _():
                pl.semaphore_wait(ready_sem.at[z], 1)
                send_top(z)

            pl.when(me_z + 1 == z)(lambda: halo(2).start())

        wait_all(top_recv.at[pl.ds(0, nz - 1)], top_sem.at[1])
        top_total[...] = top_recv[...].sum(axis=0).reshape(4, 8, 128)
        for slot in (4, 5):
            start(slot)

        for slot in range(4):
            wait_recv(slot)
        parts = [side_total[h] for h in range(2)]
        found = side_maps(
            parts,
            [side_halo[0, h] for h in range(2)],
            [side_halo[1, h] for h in range(2)],
            side_halo[2, 0],
            side_halo[2, 1],
            y_factor,
        )
        for h, maps in enumerate(found):
            for i in range(3):
                maps_mate[2 * i + h] = maps[i]
                maps_out[2 * i + h] = pltpu.roll(maps[i], 4, 0)
        at = pl.ds(0, 6)
        remote(maps_mate.at[at], maps_out.at[at], maps_sem.at[0], maps_sem.at[2], mate).start()

        for slot in (4, 5):
            wait_recv(slot)
        parts = [top_total[h] for h in range(4)]
        for h, maps in enumerate(top_maps(parts, top_halo[0], top_halo[1], z_factor)):
            for i in range(3):
                (maps_out if h // 2 else maps_mate)[6 + 2 * i + h % 2] = maps[i]
        at = pl.ds(6, 6)
        remote(maps_mate.at[at], maps_out.at[at], maps_sem.at[1], maps_sem.at[3], mate).start()

        wait_all(side_recv.at[pl.ds(0, chips - 1)], side_sem.at[0])
        wait_all(top_recv.at[pl.ds(0, nz - 1)], top_sem.at[0])
        for slot in range(6):
            wait_send(slot)
        wait_all(maps_mate.at[pl.ds(0, 6)], maps_sem.at[0])
        wait_all(maps_mate.at[pl.ds(6, 6)], maps_sem.at[1])


def unpack(maps, side_out, top_out):
    for i in range(3):
        side_out[i, :, 0:128] = maps[2 * i, :4]
        side_out[i, :, 128:256] = maps[2 * i + 1, :4]
        top_out[i, 0:8, :] = maps[6 + 2 * i, :, :64]
        top_out[i, 8:16, :] = maps[7 + 2 * i, :, :64]


def solution(mesh):
    ny, nz = mesh.shape["gy"], mesh.shape["gz"]
    chips = ny // 2

    def body(density):
        rows, depth, width = density.shape

        def blocks(*count):
            return pltpu.VMEM((*count, 8, 128), jnp.float32)

        vmem = pl.BlockSpec(memory_space=pltpu.VMEM)
        maps = pl.pallas_call(
            functools.partial(kernel, ny, nz, 1.0 / math.sqrt(depth * ny), 1.0 / math.sqrt(width * nz)),
            out_shape=pltpu.VMEM((12, 8, 128), jnp.float32),
            in_specs=[pl.BlockSpec(memory_space=pltpu.HBM)],
            out_specs=vmem,
            scratch_shapes=[
                pltpu.VMEM((rows, depth, width), jnp.float32),
                blocks(chips, 2),
                blocks(chips, 2),
                blocks(chips, 2),
                blocks(2),
                blocks(3, 2),
                blocks(CHUNKS),
                blocks(2, nz, 2),
                blocks(nz, 2, 2),
                blocks(4),
                blocks(2),
                blocks(12),
                pltpu.SemaphoreType.DMA((CHUNKS,)),
                pltpu.SemaphoreType.DMA((4,)),
                pltpu.SemaphoreType.DMA((2,)),
                pltpu.SemaphoreType.DMA((2,)),
                pltpu.SemaphoreType.DMA((12,)),
                pltpu.SemaphoreType.DMA((4,)),
                pltpu.SemaphoreType.REGULAR((nz,)),
            ],
            compiler_params=pltpu.CompilerParams(
                collective_id=0, has_side_effects=True, vmem_limit_bytes=16 * 1024 * 1024
            ),
            name="views",
        )(pltpu.with_memory_space_constraint(density, pltpu.HBM))
        side, top = pl.pallas_call(
            unpack,
            out_shape=(
                jax.ShapeDtypeStruct((3, rows // ny, width), jnp.float32),
                jax.ShapeDtypeStruct((3, depth, rows // nz), jnp.float32),
            ),
            in_specs=[vmem],
            out_specs=(vmem, vmem),
            name="unpack",
        )(pltpu.with_memory_space_constraint(maps, pltpu.VMEM))
        return side, jnp.swapaxes(top, 1, 2)

    return jax.shard_map(
        body,
        mesh=mesh,
        in_specs=(P(None, "gy", "gz"),),
        out_specs=(P(None, "gy", "gz"), P(None, "gz", "gy")),
        check_vma=False,
    )
```

time: 20.2 us -> 19.3 us (0.955)
  Pallas kernels: 19.3 us -> 18.6 us
    pallas_call x1, Pallas kernels: 18.7 us -> 18 us  [body(): pl.pallas_call(functools.partial(kernel, ny, nz, 1.0 / math.sqrt(depth *...]
where the time goes in v3:
time: 19.3 us
  Pallas kernels  18.6 us (96%)
  between operations  0.64 us (3%)
    pallas_call x1, Pallas kernels, body(): pl.pallas_call(functools.partial(kernel, ny, nz, 1.0 / math.sqrt(depth *...  18 us
    pallas_call x1, Pallas kernels, body(): pl.pallas_call(unpack, out_shape=(jax.ShapeDtypeStruct((3, rows // ny, wi...  0.62 us

profile of v3, /device:TPU:1, one launch (start us, length us, event | category | flops | bytes accessed | tf_op | source)
XLA Modules:
  0.0 19.3 jit_solution(13293842421165071033)
XLA Ops:
  0.6 18.0 %views.1.maps = f32[12,8,128]{2,1,0:T(8,128)S(1)} custom-call(f32[256,16,256]{2,1,0:T(8,128)} %density.1), custom_call_target="tpu_custom_call" | custom-call | tf_op jit(solution)/shard_map/views/pallas_call | solution.py:287
  18.6 0.6 %unpack.1 = (f32[3,4,256]{2,1,0:T(4,128)}, f32[3,16,64]{2,1,0:T(8,128)}) custom-call(f32[12,8,128]{2,1,0:T(8,128)S(1)} %views.1.maps), custom_call_target="tpu_custom_call" | custom-call | tf_op jit(solution)/shard_map/unpack/pallas_call | solution.py:318

commit v4 on v3

--- a/solution.py
+++ b/solution.py
@@ -54,7 +54,7 @@
 
 def kernel(ny, nz, y_factor, z_factor, density, maps_out, cells, side_part, side_mate, side_recv, side_total, side_halo,
            top_half, top_part, top_recv, top_total, top_halo, maps_mate, load_sem, mate_sem, side_sem, top_sem, halo_sem,
-           maps_sem, ready_sem):
+           maps_sem, chunk_sem, line_sem, ready_sem):
     rows, depth, width = cells.shape
     span = rows // CHUNKS
     chips = ny // 2
@@ -88,12 +88,9 @@
         signal(barrier, mate)
         for n in range(chips):
             pl.when(chip != n)(lambda: signal(barrier, (2 * n + 1, me_z)))
-        for z in range(1, nz):
-            pl.when(me_z < z)(lambda: signal(barrier, (me_y, z)))
-
-    @pl.when(follows)
-    def _():
-        pl.semaphore_wait(barrier, 1)
+
+    for z in range(1, nz):
+        pl.when(me_z < z)(lambda: signal(barrier, (2 * chip, z)))
 
     lane = iota(1)
 
@@ -113,14 +110,46 @@
                     block = jnp.where(place == 64 * half + 8 * k + x, here, block)
         top_half[j] = block
 
-        @pl.when(follows)
-        def _():
-            at = pl.ds(j * (span // 8), span // 8)
-            remote(side_part.at[at], side_mate.at[at], mate_sem.at[0], mate_sem.at[1], lead).start()
-
         return carry
 
-    lax.fori_loop(0, CHUNKS, add, 0)
+    owners = span // 8
+
+    def hand_over(j, carry):
+        at = pl.ds(j * owners, owners)
+        remote(side_part.at[at], side_mate.at[at], mate_sem.at[0], chunk_sem.at[j], lead).start()
+        return carry
+
+    def send_side(j, carry):
+        at = pl.ds(j * owners, owners)
+        wait_all(side_mate.at[at], chunk_sem.at[j])
+        side_part[at] += side_mate[at]
+        for q in range(owners):
+            n = j * owners + q
+
+            @pl.when(chip != n)
+            def _():
+                remote(side_part.at[n], side_recv.at[chip], side_sem.at[0], side_sem.at[1], (2 * n + 1, me_z)).start()
+
+        return carry
+
+    @pl.when(follows)
+    def _():
+        add(0, 0)
+        pl.semaphore_wait(barrier, 1 + 2 * me_z)
+        signal(line_sem, lead)
+        hand_over(0, 0)
+        for z in range(nz - 1):
+            @pl.when(me_z > z)
+            def _():
+                signal(ready_sem.at[me_z], (2 * chip + 1, z))
+                signal(ready_sem.at[me_z], (2 * chip, z))
+
+        lax.fori_loop(1, CHUNKS, lambda j, carry: hand_over(j, add(j, carry)), 0)
+
+    @pl.when(leads)
+    def _():
+        lax.fori_loop(0, CHUNKS, add, 0)
+        pl.semaphore_wait(line_sem, 1)
 
     pieces = CHUNKS // nz
     packed = []
@@ -136,14 +165,29 @@
         below = packed[z - 1] if z else nothing
         around = jnp.where(lane == 64, above, jnp.where(lane == 127, below, 0.0))
         turned = jnp.where(lane == 64, pltpu.roll(above, 64, 1), jnp.where(lane == 127, pltpu.roll(below, 64, 1), 0.0))
-        top_part[core, z, 0] = jnp.where(lane < 64, here, turned)
-        top_part[core, z, 1] = jnp.where(lane < 64, pltpu.roll(here, 64, 1), around)
+        top_part[z, 0] = jnp.where(lane < 64, here, turned)
+        top_part[z, 1] = jnp.where(lane < 64, pltpu.roll(here, 64, 1), around)
+
+    def send_top(z):
+        peer = (2 * chip + 1, z)
+        remote(top_part.at[z], top_recv.at[2 * me_z + core], top_sem.at[0], top_sem.at[1], peer).start()
+
+    def send_up():
+        for z in range(1, nz):
+            @pl.when(me_z < z)
+            def _():
+                pl.semaphore_wait(ready_sem.at[z], 1)
+                send_top(z)
+
+    for z in range(nz - 1):
+        pl.when(me_z > z)(lambda: send_top(z))
 
     @pl.when(follows)
     def _():
-        remote(top_part.at[0], top_part.at[0], mate_sem.at[2], mate_sem.at[3], lead).start()
+        send_top(me_z)
+        send_up()
         wait_all(side_part, mate_sem.at[0])
-        wait_all(top_part.at[0], mate_sem.at[2])
+        wait_all(top_part, top_sem.at[0])
         wait_all(maps_out.at[pl.ds(0, 6)], maps_sem.at[2])
         wait_all(maps_out.at[pl.ds(6, 6)], maps_sem.at[3])
 
@@ -174,10 +218,6 @@
         def wait_send(slot):
             pl.when(edges[slot % 4][0])(lambda: halo(slot).wait_send())
 
-        def send_top(z):
-            for c in range(2):
-                remote(top_part.at[c, z], top_recv.at[me_z, c], top_sem.at[0], top_sem.at[1], (me_y, z)).start()
-
         @pl.when(jnp.logical_not(edges[0][2]))
         def _():
             side_halo[0] = jnp.zeros((2, 8, 128), jnp.float32)
@@ -196,37 +236,22 @@
         def _():
             side_halo[2, 1] = nothing
 
-        pl.semaphore_wait(barrier, chips - 1 + me_z)
-        for z in range(nz - 1):
-            pl.when(me_z > z)(lambda: signal(ready_sem.at[me_z], (me_y, z)))
-        wait_all(top_part.at[0], mate_sem.at[3])
-        for z in range(nz - 1):
-            pl.when(me_z > z)(lambda: send_top(z))
-        wait_all(side_mate, mate_sem.at[1])
-        side_part[...] += side_mate[...]
-        for n in range(chips):
-            @pl.when(chip != n)
-            def _():
-                remote(side_part.at[n], side_recv.at[chip], side_sem.at[0], side_sem.at[1], (2 * n + 1, me_z)).start()
-
+        pl.semaphore_wait(barrier, chips - 1)
+        lax.fori_loop(0, CHUNKS, send_side, 0)
+        send_up()
         side_recv[chip] = side_part[chip]
-        top_recv[me_z, 0] = top_part[0, me_z]
-        top_recv[me_z, 1] = top_part[1, me_z]
+        top_recv[2 * me_z + 1] = top_part[me_z]
 
         wait_all(side_recv.at[pl.ds(0, chips - 1)], side_sem.at[1])
         side_total[...] = side_recv[...].sum(axis=0)
-        for slot in (3, 0, 1):
+        for slot in (3, 0, 1, 2):
             start(slot)
-        for z in range(1, nz):
-            @pl.when(me_z < z)
-            def _():
-                pl.semaphore_wait(ready_sem.at[z], 1)
-                send_top(z)
-
-            pl.when(me_z + 1 == z)(lambda: halo(2).start())
-
-        wait_all(top_recv.at[pl.ds(0, nz - 1)], top_sem.at[1])
-        top_total[...] = top_recv[...].sum(axis=0).reshape(4, 8, 128)
+        wait_all(top_recv.at[pl.ds(0, 2 * nz - 1)], top_sem.at[1])
+        for h in range(4):
+            added = top_recv[h // 2, h % 2]
+            for z in range(1, nz):
+                added += top_recv[2 * z + h // 2, h % 2]
+            top_total[h] = added
         for slot in (4, 5):
             start(slot)
 
@@ -258,7 +283,7 @@
         remote(maps_mate.at[at], maps_out.at[at], maps_sem.at[1], maps_sem.at[3], mate).start()
 
         wait_all(side_recv.at[pl.ds(0, chips - 1)], side_sem.at[0])
-        wait_all(top_recv.at[pl.ds(0, nz - 1)], top_sem.at[0])
+        wait_all(top_part.at[pl.ds(0, nz - 1)], top_sem.at[0])
         for slot in range(6):
             wait_send(slot)
         wait_all(maps_mate.at[pl.ds(0, 6)], maps_sem.at[0])
@@ -297,17 +322,19 @@
                 blocks(2),
                 blocks(3, 2),
                 blocks(CHUNKS),
-                blocks(2, nz, 2),
-                blocks(nz, 2, 2),
+                blocks(nz, 2),
+                blocks(2 * nz, 2),
                 blocks(4),
                 blocks(2),
                 blocks(12),
                 pltpu.SemaphoreType.DMA((CHUNKS,)),
-                pltpu.SemaphoreType.DMA((4,)),
+                pltpu.SemaphoreType.DMA((1,)),
                 pltpu.SemaphoreType.DMA((2,)),
                 pltpu.SemaphoreType.DMA((2,)),
                 pltpu.SemaphoreType.DMA((12,)),
                 pltpu.SemaphoreType.DMA((4,)),
+                pltpu.SemaphoreType.DMA((CHUNKS,)),
+                pltpu.SemaphoreType.REGULAR,
                 pltpu.SemaphoreType.REGULAR((nz,)),
             ],
             compiler_params=pltpu.CompilerParams(

time: 19.3 us -> 18.2 us (0.943)
  Pallas kernels: 18.6 us -> 17.5 us
    pallas_call x1, Pallas kernels: 18 us -> 16.8 us  [body(): pl.pallas_call(functools.partial(kernel, ny, nz, 1.0 / math.sqrt(depth *...]
where the time goes in v4:
time: 18.2 us; the launch traced here: 18.1 us
  Pallas kernels  17.5 us (96%)
  between operations  0.64 us (4%)
    pallas_call x1, Pallas kernels, body(): pl.pallas_call(functools.partial(kernel, ny, nz, 1.0 / math.sqrt(depth *...  16.8 us
    pallas_call x1, Pallas kernels, body(): pl.pallas_call(unpack, out_shape=(jax.ShapeDtypeStruct((3, rows // ny, wi...  0.62 us

profile of v4, /device:TPU:1, one launch (start us, length us, event | category | flops | bytes accessed | tf_op | source)
XLA Modules:
  0.0 18.1 jit_solution(15923244717165239867)
XLA Ops:
  0.6 16.8 %views.1.maps = f32[12,8,128]{2,1,0:T(8,128)S(1)} custom-call(f32[256,16,256]{2,1,0:T(8,128)} %density.1), custom_call_target="tpu_custom_call" | custom-call | tf_op jit(solution)/shard_map/views/pallas_call | solution.py:312
  17.5 0.6 %unpack.1 = (f32[3,4,256]{2,1,0:T(4,128)}, f32[3,16,64]{2,1,0:T(8,128)}) custom-call(f32[12,8,128]{2,1,0:T(8,128)S(1)} %views.1.maps), custom_call_target="tpu_custom_call" | custom-call | tf_op jit(solution)/shard_map/unpack/pallas_call | solution.py:345

commit v5 on v4

--- a/solution.py
+++ b/solution.py
@@ -38,9 +38,9 @@
         )
 
 
-def top_maps(parts, low_y, high_y, factor):
+def top_maps(below, parts, above, factor):
     row = iota(0)
-    around = (low_y, *parts, high_y)
+    around = (below, *parts, above)
     for h, here in enumerate(parts):
         yield stencil(
             here,
@@ -53,8 +53,8 @@
 
 
 def kernel(ny, nz, y_factor, z_factor, density, maps_out, cells, side_part, side_mate, side_recv, side_total, side_halo,
-           top_half, top_part, top_recv, top_total, top_halo, maps_mate, load_sem, mate_sem, side_sem, top_sem, halo_sem,
-           maps_sem, chunk_sem, line_sem, ready_sem):
+           top_half, top_part, top_recv, top_total, top_halo, load_sem, mate_sem, side_sem, top_sem, edge_sem, chunk_sem,
+           line_sem, ready_sem):
     rows, depth, width = cells.shape
     span = rows // CHUNKS
     chips = ny // 2
@@ -182,60 +182,67 @@
     for z in range(nz - 1):
         pl.when(me_z > z)(lambda: send_top(z))
 
+    up, down = 2 * chip + 3, 2 * chip - 1
+    totals = (
+        (side_total, side_halo.at[0], chip < chips - 1, chip > 0, (up - 1, me_z)),
+        (side_total, side_halo.at[0], chip > 0, chip < chips - 1, (down, me_z)),
+        (side_total.at[1], side_halo.at[1, 0], me_z < nz - 1, me_z > 0, (me_y, me_z + 1)),
+        (side_total.at[0], side_halo.at[1, 1], me_z > 0, me_z < nz - 1, (me_y, me_z - 1)),
+        (side_total.at[1], side_halo.at[1, 0], me_z < nz - 1, me_z > 0, (2 * chip, me_z + 1)),
+        (side_total.at[0], side_halo.at[1, 1], me_z > 0, me_z < nz - 1, (2 * chip, me_z - 1)),
+        (side_total, side_total, leads, follows, mate),
+        (top_total.at[3], top_halo, chip < chips - 1, chip > 0, (up - 1, me_z)),
+        (top_total.at[0], top_halo, chip > 0, chip < chips - 1, (down, me_z)),
+        (top_total, top_total, leads, follows, mate),
+    )
+
+    def total(k):
+        src, dst, _, _, peer = totals[k]
+        return remote(src, dst, edge_sem.at[k], edge_sem.at[len(totals) + k], peer)
+
+    def send_totals(*which):
+        for k in which:
+            pl.when(totals[k][2])(lambda: total(k).start())
+
+    def wait_totals(*which):
+        for k in which:
+            pl.when(totals[k][3])(lambda: total(k).wait_recv())
+
+    for h, missing in enumerate((me_z == 0, me_z == nz - 1)):
+        @pl.when(missing)
+        def _():
+            side_halo[1, h] = nothing
+
+    @pl.when(me_y % (ny - 1) == 0)
+    def _():
+        side_halo[0] = jnp.zeros((2, 8, 128), jnp.float32)
+        top_halo[...] = nothing
+
+    def make_side(shift):
+        beside = [side_halo[0, h] for h in range(2)]
+        parts = [side_total[h] for h in range(2)]
+        for h, maps in enumerate(side_maps(parts, beside, beside, side_halo[1, 0], side_halo[1, 1], y_factor)):
+            for i in range(3):
+                maps_out[2 * i + h] = pltpu.roll(maps[i], 4, 0) if shift else maps[i]
+
+    def make_top(below, parts, above):
+        for h, maps in enumerate(top_maps(below, parts, above, z_factor)):
+            for i in range(3):
+                maps_out[6 + 2 * i + h] = maps[i]
+
     @pl.when(follows)
     def _():
         send_top(me_z)
         send_up()
         wait_all(side_part, mate_sem.at[0])
         wait_all(top_part, top_sem.at[0])
-        wait_all(maps_out.at[pl.ds(0, 6)], maps_sem.at[2])
-        wait_all(maps_out.at[pl.ds(6, 6)], maps_sem.at[3])
+        wait_totals(6, 0, 4, 5)
+        make_side(False)
+        wait_totals(9, 7)
+        make_top(top_halo[...], [top_total[0], top_total[1]], top_total[2])
 
     @pl.when(leads)
     def _():
-        edges = (
-            (chip < chips - 1, (me_y + 2, me_z), chip > 0),
-            (chip > 0, (me_y - 2, me_z), chip < chips - 1),
-            (me_z < nz - 1, (me_y, me_z + 1), me_z > 0),
-            (me_z > 0, (me_y, me_z - 1), me_z < nz - 1),
-        )
-
-        def halo(slot):
-            if slot < 2:
-                src, dst = side_total, side_halo.at[slot]
-            elif slot < 4:
-                src, dst = side_total.at[3 - slot], side_halo.at[2, slot - 2]
-            else:
-                src, dst = top_total.at[3 * (5 - slot)], top_halo.at[slot - 4]
-            return remote(src, dst, halo_sem.at[slot], halo_sem.at[6 + slot], edges[slot % 4][1])
-
-        def start(slot):
-            pl.when(edges[slot % 4][0])(lambda: halo(slot).start())
-
-        def wait_recv(slot):
-            pl.when(edges[slot % 4][2])(lambda: halo(slot).wait_recv())
-
-        def wait_send(slot):
-            pl.when(edges[slot % 4][0])(lambda: halo(slot).wait_send())
-
-        @pl.when(jnp.logical_not(edges[0][2]))
-        def _():
-            side_halo[0] = jnp.zeros((2, 8, 128), jnp.float32)
-            top_halo[0] = nothing
-
-        @pl.when(jnp.logical_not(edges[1][2]))
-        def _():
-            side_halo[1] = jnp.zeros((2, 8, 128), jnp.float32)
-            top_halo[1] = nothing
-
-        @pl.when(jnp.logical_not(edges[2][2]))
-        def _():
-            side_halo[2, 0] = nothing
-
-        @pl.when(jnp.logical_not(edges[3][2]))
-        def _():
-            side_halo[2, 1] = nothing
-
         pl.semaphore_wait(barrier, chips - 1)
         lax.fori_loop(0, CHUNKS, send_side, 0)
         send_up()
@@ -244,50 +251,24 @@
 
         wait_all(side_recv.at[pl.ds(0, chips - 1)], side_sem.at[1])
         side_total[...] = side_recv[...].sum(axis=0)
-        for slot in (3, 0, 1, 2):
-            start(slot)
+        send_totals(3, 5, 2, 4, 1, 0, 6)
+
         wait_all(top_recv.at[pl.ds(0, 2 * nz - 1)], top_sem.at[1])
         for h in range(4):
             added = top_recv[h // 2, h % 2]
             for z in range(1, nz):
                 added += top_recv[2 * z + h // 2, h % 2]
             top_total[h] = added
-        for slot in (4, 5):
-            start(slot)
-
-        for slot in range(4):
-            wait_recv(slot)
-        parts = [side_total[h] for h in range(2)]
-        found = side_maps(
-            parts,
-            [side_halo[0, h] for h in range(2)],
-            [side_halo[1, h] for h in range(2)],
-            side_halo[2, 0],
-            side_halo[2, 1],
-            y_factor,
-        )
-        for h, maps in enumerate(found):
-            for i in range(3):
-                maps_mate[2 * i + h] = maps[i]
-                maps_out[2 * i + h] = pltpu.roll(maps[i], 4, 0)
-        at = pl.ds(0, 6)
-        remote(maps_mate.at[at], maps_out.at[at], maps_sem.at[0], maps_sem.at[2], mate).start()
-
-        for slot in (4, 5):
-            wait_recv(slot)
-        parts = [top_total[h] for h in range(4)]
-        for h, maps in enumerate(top_maps(parts, top_halo[0], top_halo[1], z_factor)):
-            for i in range(3):
-                (maps_out if h // 2 else maps_mate)[6 + 2 * i + h % 2] = maps[i]
-        at = pl.ds(6, 6)
-        remote(maps_mate.at[at], maps_out.at[at], maps_sem.at[1], maps_sem.at[3], mate).start()
+        send_totals(8, 7, 9)
 
         wait_all(side_recv.at[pl.ds(0, chips - 1)], side_sem.at[0])
         wait_all(top_part.at[pl.ds(0, nz - 1)], top_sem.at[0])
-        for slot in range(6):
-            wait_send(slot)
-        wait_all(maps_mate.at[pl.ds(0, 6)], maps_sem.at[0])
-        wait_all(maps_mate.at[pl.ds(6, 6)], maps_sem.at[1])
+        wait_totals(1, 2, 3)
+        make_side(True)
+        wait_totals(8)
+        make_top(top_total[1], [top_total[2], top_total[3]], top_halo[...])
+        for k in range(len(totals)):
+            pl.when(totals[k][2])(lambda: total(k).wait_send())
 
 
 def unpack(maps, side_out, top_out):
@@ -320,19 +301,17 @@
                 blocks(chips, 2),
                 blocks(chips, 2),
                 blocks(2),
-                blocks(3, 2),
+                blocks(2, 2),
                 blocks(CHUNKS),
                 blocks(nz, 2),
                 blocks(2 * nz, 2),
                 blocks(4),
-                blocks(2),
-                blocks(12),
+                blocks(),
                 pltpu.SemaphoreType.DMA((CHUNKS,)),
                 pltpu.SemaphoreType.DMA((1,)),
                 pltpu.SemaphoreType.DMA((2,)),
                 pltpu.SemaphoreType.DMA((2,)),
-                pltpu.SemaphoreType.DMA((12,)),
-                pltpu.SemaphoreType.DMA((4,)),
+                pltpu.SemaphoreType.DMA((20,)),
                 pltpu.SemaphoreType.DMA((CHUNKS,)),
                 pltpu.SemaphoreType.REGULAR,
                 pltpu.SemaphoreType.REGULAR((nz,)),

time: 18.2 us -> 17.4 us (0.956)
  Pallas kernels: 17.5 us -> 16.6 us
    pallas_call x1, Pallas kernels: 16.8 us -> 16 us  [body(): pl.pallas_call(functools.partial(kernel, ny, nz, 1.0 / math.sqrt(depth *...]
where the time goes in v5:
time: 17.4 us; the launch traced here: 17.3 us
  Pallas kernels  16.6 us (95%)
  between operations  0.64 us (4%)
    pallas_call x1, Pallas kernels, body(): pl.pallas_call(functools.partial(kernel, ny, nz, 1.0 / math.sqrt(depth *...  16 us
    pallas_call x1, Pallas kernels, body(): pl.pallas_call(unpack, out_shape=(jax.ShapeDtypeStruct((3, rows // ny, wi...  0.62 us

profile of v5, /device:TPU:1, one launch (start us, length us, event | category | flops | bytes accessed | tf_op | source)
XLA Modules:
  0.0 17.3 jit_solution(14916795648933375743)
XLA Ops:
  0.6 16.0 %views.1.maps = f32[12,8,128]{2,1,0:T(8,128)S(1)} custom-call(f32[256,16,256]{2,1,0:T(8,128)} %density.1), custom_call_target="tpu_custom_call" | custom-call | tf_op jit(solution)/shard_map/views/pallas_call | solution.py:293
  16.7 0.6 %unpack.1 = (f32[3,4,256]{2,1,0:T(4,128)}, f32[3,16,64]{2,1,0:T(8,128)}) custom-call(f32[12,8,128]{2,1,0:T(8,128)S(1)} %views.1.maps), custom_call_target="tpu_custom_call" | custom-call | tf_op jit(solution)/shard_map/unpack/pallas_call | solution.py:324

commit v6 on v5

--- a/solution.py
+++ b/solution.py
@@ -10,6 +10,7 @@
 
 MESH = pl.DeviceIdType.MESH
 CHUNKS = 8
+LOADS = 8
 
 
 def iota(axis):
@@ -53,22 +54,23 @@
 
 
 def kernel(ny, nz, y_factor, z_factor, density, maps_out, cells, side_part, side_mate, side_recv, side_total, side_halo,
-           top_half, top_part, top_recv, top_total, top_halo, load_sem, mate_sem, side_sem, top_sem, edge_sem, chunk_sem,
-           line_sem, ready_sem):
+           top_half, top_part, top_recv, top_total, top_halo, load_sem, chunk_sem, out_sem, side_sem, top_sem, edge_out,
+           edge_in, line_sem, ready_sem):
     rows, depth, width = cells.shape
     span = rows // CHUNKS
     chips = ny // 2
+    tiles = depth * width // 1024
     me_y, me_z = lax.axis_index("gy"), lax.axis_index("gz")
     chip, core = me_y // 2, me_y % 2
     leads, follows = core == 1, core == 0
     lead, mate = (2 * chip + 1, me_z), (2 * chip, me_z)
 
-    def load(j):
-        at = pl.ds(j * span, span)
-        return pltpu.make_async_copy(density.at[at], cells.at[at], load_sem.at[j])
-
-    for j in range(CHUNKS):
-        load(j).start()
+    def load(i):
+        at = pl.ds(i * (rows // LOADS), rows // LOADS)
+        return pltpu.make_async_copy(density.at[at], cells.at[at], load_sem.at[i])
+
+    for i in range(LOADS):
+        load(i).start()
 
     def remote(src, dst, send, recv, peer):
         return pltpu.make_async_remote_copy(
@@ -94,8 +96,8 @@
 
     lane = iota(1)
 
-    def add(j, carry):
-        load(j).wait()
+    def add(j):
+        pl.when(j % (CHUNKS // LOADS) == 0)(lambda: load(j // (CHUNKS // LOADS)).wait())
         block = jnp.zeros((8, 128), jnp.float32)
         place = lane - (j * span) % 64
         for k in range(span // 8):
@@ -110,95 +112,102 @@
                     block = jnp.where(place == 64 * half + 8 * k + x, here, block)
         top_half[j] = block
 
-        return carry
 
     owners = span // 8
-
-    def hand_over(j, carry):
+    nothing = jnp.zeros((8, 128), jnp.float32)
+
+    def hand_over(j):
         at = pl.ds(j * owners, owners)
-        remote(side_part.at[at], side_mate.at[at], mate_sem.at[0], chunk_sem.at[j], lead).start()
-        return carry
+        remote(side_part.at[at], side_mate.at[at], out_sem, chunk_sem.at[(j + 3) // 4], lead).start()
 
     def send_side(j, carry):
+        for lot, first, end in ((0, 0, 1), (1, 1, 5), (2, 5, CHUNKS)):
+            pl.when(j == first)(
+                lambda: wait_all(side_mate.at[pl.ds(first * owners, (end - first) * owners)], chunk_sem.at[lot])
+            )
         at = pl.ds(j * owners, owners)
-        wait_all(side_mate.at[at], chunk_sem.at[j])
         side_part[at] += side_mate[at]
         for q in range(owners):
             n = j * owners + q
 
             @pl.when(chip != n)
             def _():
-                remote(side_part.at[n], side_recv.at[chip], side_sem.at[0], side_sem.at[1], (2 * n + 1, me_z)).start()
+                remote(side_part.at[n], side_recv.at[chip], out_sem, side_sem, (2 * n + 1, me_z)).start()
 
         return carry
 
-    @pl.when(follows)
-    def _():
-        add(0, 0)
-        pl.semaphore_wait(barrier, 1 + 2 * me_z)
-        signal(line_sem, lead)
-        hand_over(0, 0)
-        for z in range(nz - 1):
-            @pl.when(me_z > z)
-            def _():
-                signal(ready_sem.at[me_z], (2 * chip + 1, z))
-                signal(ready_sem.at[me_z], (2 * chip, z))
-
-        lax.fori_loop(1, CHUNKS, lambda j, carry: hand_over(j, add(j, carry)), 0)
-
-    @pl.when(leads)
-    def _():
-        lax.fori_loop(0, CHUNKS, add, 0)
-        pl.semaphore_wait(line_sem, 1)
-
-    pieces = CHUNKS // nz
-    packed = []
-    for z in range(nz):
-        block = top_half[pieces * z]
-        for i in range(1, pieces):
-            block += top_half[pieces * z + i]
-        packed.append(block)
-    nothing = jnp.zeros((8, 128), jnp.float32)
-    for z in range(nz):
-        here = packed[z]
-        above = packed[z + 1] if z + 1 < nz else nothing
-        below = packed[z - 1] if z else nothing
+    def send_top(z):
+        remote(top_part.at[z], top_recv.at[2 * me_z + core], out_sem, top_sem, (2 * chip + 1, z)).start()
+
+    def pack(z, above):
+        here = top_half[2 * z] + top_half[2 * z + 1]
+        below = jnp.where(z > 0, top_half[jnp.maximum(2 * z - 1, 0)], 0.0)
         around = jnp.where(lane == 64, above, jnp.where(lane == 127, below, 0.0))
         turned = jnp.where(lane == 64, pltpu.roll(above, 64, 1), jnp.where(lane == 127, pltpu.roll(below, 64, 1), 0.0))
         top_part[z, 0] = jnp.where(lane < 64, here, turned)
         top_part[z, 1] = jnp.where(lane < 64, pltpu.roll(here, 64, 1), around)
 
-    def send_top(z):
-        peer = (2 * chip + 1, z)
-        remote(top_part.at[z], top_recv.at[2 * me_z + core], top_sem.at[0], top_sem.at[1], peer).start()
+    def step(j, carry):
+        add(j)
+
+        @pl.when(follows)
+        def _():
+            @pl.when(j == 0)
+            def _():
+                pl.semaphore_wait(barrier, 1 + 2 * me_z)
+                signal(line_sem, lead)
+
+            hand_over(j)
+
+            @pl.when(j == 0)
+            def _():
+                for z in range(nz - 1):
+                    @pl.when(me_z > z)
+                    def _():
+                        signal(ready_sem, (2 * chip + 1, z))
+                        signal(ready_sem, (2 * chip, z))
+
+        @pl.when(jnp.logical_and(j >= 2, j % 2 == 0))
+        def _():
+            z = j // 2 - 1
+            pack(z, top_half[j])
+            pl.when(jnp.logical_and(leads, z == 0))(lambda: pl.semaphore_wait(line_sem, 1))
+            pl.when(z < me_z)(lambda: send_top(z))
+
+        return carry
+
+    lax.fori_loop(0, CHUNKS - 1, step, 0)
+
+    @pl.when(leads)
+    def _():
+        pl.semaphore_wait(barrier, chips - 1)
+        lax.fori_loop(0, 2, send_side, 0)
+
+    lax.fori_loop(CHUNKS - 1, CHUNKS, step, 0)
 
     def send_up():
+        pl.when(me_z < nz - 1)(lambda: pl.semaphore_wait(ready_sem, nz - 1 - me_z))
         for z in range(1, nz):
-            @pl.when(me_z < z)
-            def _():
-                pl.semaphore_wait(ready_sem.at[z], 1)
-                send_top(z)
-
-    for z in range(nz - 1):
-        pl.when(me_z > z)(lambda: send_top(z))
+            pl.when(me_z < z)(lambda: send_top(z))
 
     up, down = 2 * chip + 3, 2 * chip - 1
+    last, top = chip == chips - 1, me_z == nz - 1
     totals = (
-        (side_total, side_halo.at[0], chip < chips - 1, chip > 0, (up - 1, me_z)),
-        (side_total, side_halo.at[0], chip > 0, chip < chips - 1, (down, me_z)),
-        (side_total.at[1], side_halo.at[1, 0], me_z < nz - 1, me_z > 0, (me_y, me_z + 1)),
-        (side_total.at[0], side_halo.at[1, 1], me_z > 0, me_z < nz - 1, (me_y, me_z - 1)),
-        (side_total.at[1], side_halo.at[1, 0], me_z < nz - 1, me_z > 0, (2 * chip, me_z + 1)),
-        (side_total.at[0], side_halo.at[1, 1], me_z > 0, me_z < nz - 1, (2 * chip, me_z - 1)),
-        (side_total, side_total, leads, follows, mate),
-        (top_total.at[3], top_halo, chip < chips - 1, chip > 0, (up - 1, me_z)),
-        (top_total.at[0], top_halo, chip > 0, chip < chips - 1, (down, me_z)),
-        (top_total, top_total, leads, follows, mate),
+        (side_total, side_halo.at[0], ~last, chip > 0, (up - 1, me_z), 0, edge_in.at[0]),
+        (side_total, side_halo.at[0], chip > 0, ~last, (down, me_z), 1, edge_in.at[0]),
+        (side_total.at[1], side_halo.at[1, 0], ~top, me_z > 0, (me_y, me_z + 1), 2, edge_in.at[1]),
+        (side_total.at[0], side_halo.at[1, 1], me_z > 0, ~top, (me_y, me_z - 1), 3, edge_in.at[2]),
+        (side_total.at[1], side_halo.at[1, 0], ~top, me_z > 0, (2 * chip, me_z + 1), 2, edge_in.at[1]),
+        (side_total.at[0], side_halo.at[1, 1], me_z > 0, ~top, (2 * chip, me_z - 1), 3, edge_in.at[2]),
+        (side_total, side_total, leads, follows, mate, 4, side_sem),
+        (top_total.at[3], top_halo, ~last, chip > 0, (up - 1, me_z), 0, edge_in.at[3]),
+        (top_total.at[0], top_halo, chip > 0, ~last, (down, me_z), 1, edge_in.at[3]),
+        (top_total, top_total, leads, follows, mate, 4, top_sem),
     )
 
     def total(k):
-        src, dst, _, _, peer = totals[k]
-        return remote(src, dst, edge_sem.at[k], edge_sem.at[len(totals) + k], peer)
+        src, dst, _, _, peer, send, recv = totals[k]
+        return remote(src, dst, edge_out.at[send], recv, peer)
 
     def send_totals(*which):
         for k in which:
@@ -232,28 +241,28 @@
 
     @pl.when(follows)
     def _():
+        pack(nz - 1, nothing)
         send_top(me_z)
         send_up()
-        wait_all(side_part, mate_sem.at[0])
-        wait_all(top_part, top_sem.at[0])
         wait_totals(6, 0, 4, 5)
         make_side(False)
         wait_totals(9, 7)
         make_top(top_halo[...], [top_total[0], top_total[1]], top_total[2])
+        wait_all(cells.at[pl.ds(0, (2 * chips + 2 * nz) // tiles)], out_sem)
 
     @pl.when(leads)
     def _():
-        pl.semaphore_wait(barrier, chips - 1)
-        lax.fori_loop(0, CHUNKS, send_side, 0)
+        lax.fori_loop(2, CHUNKS, send_side, 0)
+        pack(nz - 1, nothing)
         send_up()
         side_recv[chip] = side_part[chip]
         top_recv[2 * me_z + 1] = top_part[me_z]
 
-        wait_all(side_recv.at[pl.ds(0, chips - 1)], side_sem.at[1])
+        wait_all(side_recv.at[pl.ds(0, chips - 1)], side_sem)
         side_total[...] = side_recv[...].sum(axis=0)
         send_totals(3, 5, 2, 4, 1, 0, 6)
 
-        wait_all(top_recv.at[pl.ds(0, 2 * nz - 1)], top_sem.at[1])
+        wait_all(top_recv.at[pl.ds(0, 2 * nz - 1)], top_sem)
         for h in range(4):
             added = top_recv[h // 2, h % 2]
             for z in range(1, nz):
@@ -261,14 +270,14 @@
             top_total[h] = added
         send_totals(8, 7, 9)
 
-        wait_all(side_recv.at[pl.ds(0, chips - 1)], side_sem.at[0])
-        wait_all(top_part.at[pl.ds(0, nz - 1)], top_sem.at[0])
+        wait_all(cells.at[pl.ds(0, (2 * (chips - 1) + 2 * (nz - 1)) // tiles)], out_sem)
+        wait_totals(8)
+        make_top(top_total[1], [top_total[2], top_total[3]], top_halo[...])
+        for send, (out, count) in enumerate(((~last, 3), (chip > 0, 3), (~top, 2), (me_z > 0, 2))):
+            pl.when(out)(lambda: wait_all(top_total.at[pl.ds(0, count)], edge_out.at[send]))
+        wait_all(top_part.at[pl.ds(0, 3)], edge_out.at[4])
         wait_totals(1, 2, 3)
         make_side(True)
-        wait_totals(8)
-        make_top(top_total[1], [top_total[2], top_total[3]], top_halo[...])
-        for k in range(len(totals)):
-            pl.when(totals[k][2])(lambda: total(k).wait_send())
 
 
 def unpack(maps, side_out, top_out):
@@ -307,14 +316,15 @@
                 blocks(2 * nz, 2),
                 blocks(4),
                 blocks(),
-                pltpu.SemaphoreType.DMA((CHUNKS,)),
-                pltpu.SemaphoreType.DMA((1,)),
-                pltpu.SemaphoreType.DMA((2,)),
-                pltpu.SemaphoreType.DMA((2,)),
-                pltpu.SemaphoreType.DMA((20,)),
-                pltpu.SemaphoreType.DMA((CHUNKS,)),
+                pltpu.SemaphoreType.DMA((LOADS,)),
+                pltpu.SemaphoreType.DMA((3,)),
+                pltpu.SemaphoreType.DMA,
+                pltpu.SemaphoreType.DMA,
+                pltpu.SemaphoreType.DMA,
+                pltpu.SemaphoreType.DMA((5,)),
+                pltpu.SemaphoreType.DMA((4,)),
                 pltpu.SemaphoreType.REGULAR,
-                pltpu.SemaphoreType.REGULAR((nz,)),
+                pltpu.SemaphoreType.REGULAR,
             ],
             compiler_params=pltpu.CompilerParams(
                 collective_id=0, has_side_effects=True, vmem_limit_bytes=16 * 1024 * 1024

time: 17.4 us -> 17.1 us (0.983)
  Pallas kernels: 16.6 us -> 16.3 us
    pallas_call x1, Pallas kernels: 16 us -> 15.7 us  [body(): pl.pallas_call(functools.partial(kernel, ny, nz, 1.0 / math.sqrt(depth *...]
where the time goes in v6:
time: 17.1 us; the launch traced here: 17 us
  Pallas kernels  16.3 us (95%)
  between operations  0.64 us (4%)
    pallas_call x1, Pallas kernels, body(): pl.pallas_call(functools.partial(kernel, ny, nz, 1.0 / math.sqrt(depth *...  15.7 us
    pallas_call x1, Pallas kernels, body(): pl.pallas_call(unpack, out_shape=(jax.ShapeDtypeStruct((3, rows // ny, wi...  0.62 us

profile of v6, /device:TPU:1, one launch (start us, length us, event | category | flops | bytes accessed | tf_op | source)
XLA Modules:
  0.0 17.0 jit_solution(18386977955295924368)
XLA Ops:
  0.6 15.7 %views.1.maps = f32[12,8,128]{2,1,0:T(8,128)S(1)} custom-call(f32[256,16,256]{2,1,0:T(8,128)} %density.1), custom_call_target="tpu_custom_call" | custom-call | tf_op jit(solution)/shard_map/views/pallas_call | solution.py:302
  16.4 0.6 %unpack.1 = (f32[3,4,256]{2,1,0:T(4,128)}, f32[3,16,64]{2,1,0:T(8,128)}) custom-call(f32[12,8,128]{2,1,0:T(8,128)S(1)} %views.1.maps), custom_call_target="tpu_custom_call" | custom-call | tf_op jit(solution)/shard_map/unpack/pallas_call | solution.py:334

commit v7 on v6

--- a/solution.py
+++ b/solution.py
@@ -53,7 +53,7 @@
         )
 
 
-def kernel(ny, nz, y_factor, z_factor, density, maps_out, cells, side_part, side_mate, side_recv, side_total, side_halo,
+def kernel(ny, nz, y_factor, z_factor, density, maps_out, cells, side_part, side_mate, side_recv, side_total, side_halo, side_low, side_high, edge_part, edge_recv,
            top_half, top_part, top_recv, top_total, top_halo, load_sem, chunk_sem, out_sem, side_sem, top_sem, edge_out,
            edge_in, line_sem, ready_sem):
     rows, depth, width = cells.shape
@@ -90,6 +90,11 @@
         signal(barrier, mate)
         for n in range(chips):
             pl.when(chip != n)(lambda: signal(barrier, (2 * n + 1, me_z)))
+
+        @pl.when(me_z < nz - 1)
+        def _():
+            for n in range(chips):
+                signal(barrier, (2 * n + 1, me_z + 1))
 
     for z in range(1, nz):
         pl.when(me_z < z)(lambda: signal(barrier, (2 * chip, z)))
@@ -127,6 +132,15 @@
             )
         at = pl.ds(j * owners, owners)
         side_part[at] += side_mate[at]
+        @pl.when(me_z > 0)
+        def _():
+            columns = jnp.broadcast_to(side_part[at, 0][:, :, :1], (owners, 8, 128))
+            edge_part[at, 0:1] = jnp.where((iota(0) == lane)[None], columns, 0.0).sum(axis=1, keepdims=True)
+            for q in range(owners):
+                n = j * owners + q
+                src, dst = edge_part.at[n, pl.ds(0, 1)], edge_recv.at[chip, pl.ds(0, 1)]
+                remote(src, dst, out_sem, edge_in.at[2], (2 * n + 1, me_z - 1)).start()
+
         for q in range(owners):
             n = j * owners + q
 
@@ -180,7 +194,8 @@
 
     @pl.when(leads)
     def _():
-        pl.semaphore_wait(barrier, chips - 1)
+        pl.when(me_z == 0)(lambda: pl.semaphore_wait(barrier, chips - 1))
+        pl.when(me_z > 0)(lambda: pl.semaphore_wait(barrier, 2 * chips - 1))
         lax.fori_loop(0, 2, send_side, 0)
 
     lax.fori_loop(CHUNKS - 1, CHUNKS, step, 0)
@@ -193,12 +208,11 @@
     up, down = 2 * chip + 3, 2 * chip - 1
     last, top = chip == chips - 1, me_z == nz - 1
     totals = (
-        (side_total, side_halo.at[0], ~last, chip > 0, (up - 1, me_z), 0, edge_in.at[0]),
-        (side_total, side_halo.at[0], chip > 0, ~last, (down, me_z), 1, edge_in.at[0]),
-        (side_total.at[1], side_halo.at[1, 0], ~top, me_z > 0, (me_y, me_z + 1), 2, edge_in.at[1]),
-        (side_total.at[0], side_halo.at[1, 1], me_z > 0, ~top, (me_y, me_z - 1), 3, edge_in.at[2]),
-        (side_total.at[1], side_halo.at[1, 0], ~top, me_z > 0, (2 * chip, me_z + 1), 2, edge_in.at[1]),
-        (side_total.at[0], side_halo.at[1, 1], me_z > 0, ~top, (2 * chip, me_z - 1), 3, edge_in.at[2]),
+        (side_total, side_halo, ~last, chip > 0, (up - 1, me_z), 0, edge_in.at[0]),
+        (side_total, side_halo, chip > 0, ~last, (down, me_z), 1, edge_in.at[0]),
+        (side_total.at[1], side_low, ~top, me_z > 0, (me_y, me_z + 1), 2, edge_in.at[1]),
+        (side_total.at[1], side_low, ~top, me_z > 0, (2 * chip, me_z + 1), 2, edge_in.at[1]),
+        (side_high, side_high, ~top, ~top, mate, 3, edge_in.at[2]),
         (side_total, side_total, leads, follows, mate, 4, side_sem),
         (top_total.at[3], top_halo, ~last, chip > 0, (up - 1, me_z), 0, edge_in.at[3]),
         (top_total.at[0], top_halo, chip > 0, ~last, (down, me_z), 1, edge_in.at[3]),
@@ -217,20 +231,23 @@
         for k in which:
             pl.when(totals[k][3])(lambda: total(k).wait_recv())
 
-    for h, missing in enumerate((me_z == 0, me_z == nz - 1)):
-        @pl.when(missing)
-        def _():
-            side_halo[1, h] = nothing
+    @pl.when(me_z == 0)
+    def _():
+        side_low[...] = nothing
+
+    @pl.when(top)
+    def _():
+        side_high[...] = nothing
 
     @pl.when(me_y % (ny - 1) == 0)
     def _():
-        side_halo[0] = jnp.zeros((2, 8, 128), jnp.float32)
+        side_halo[...] = jnp.zeros((2, 8, 128), jnp.float32)
         top_halo[...] = nothing
 
     def make_side(shift):
-        beside = [side_halo[0, h] for h in range(2)]
+        beside = [side_halo[h] for h in range(2)]
         parts = [side_total[h] for h in range(2)]
-        for h, maps in enumerate(side_maps(parts, beside, beside, side_halo[1, 0], side_halo[1, 1], y_factor)):
+        for h, maps in enumerate(side_maps(parts, beside, beside, side_low[...], side_high[...], y_factor)):
             for i in range(3):
                 maps_out[2 * i + h] = pltpu.roll(maps[i], 4, 0) if shift else maps[i]
 
@@ -244,10 +261,10 @@
         pack(nz - 1, nothing)
         send_top(me_z)
         send_up()
-        wait_totals(6, 0, 4, 5)
+        wait_totals(8, 6)
+        make_top(top_halo[...], [top_total[0], top_total[1]], top_total[2])
+        wait_totals(5, 0, 3, 4)
         make_side(False)
-        wait_totals(9, 7)
-        make_top(top_halo[...], [top_total[0], top_total[1]], top_total[2])
         wait_all(cells.at[pl.ds(0, (2 * chips + 2 * nz) // tiles)], out_sem)
 
     @pl.when(leads)
@@ -260,7 +277,7 @@
 
         wait_all(side_recv.at[pl.ds(0, chips - 1)], side_sem)
         side_total[...] = side_recv[...].sum(axis=0)
-        send_totals(3, 5, 2, 4, 1, 0, 6)
+        send_totals(2, 3, 1, 0, 5)
 
         wait_all(top_recv.at[pl.ds(0, 2 * nz - 1)], top_sem)
         for h in range(4):
@@ -268,16 +285,27 @@
             for z in range(1, nz):
                 added += top_recv[2 * z + h // 2, h % 2]
             top_total[h] = added
-        send_totals(8, 7, 9)
-
-        wait_all(cells.at[pl.ds(0, (2 * (chips - 1) + 2 * (nz - 1)) // tiles)], out_sem)
-        wait_totals(8)
+        send_totals(7, 6, 8)
+
+        @pl.when(~top)
+        def _():
+            wait_all(edge_recv.at[pl.ds(0, chips), pl.ds(0, 1)], edge_in.at[2])
+            column = jnp.broadcast_to(edge_recv[:, 0:1].sum(axis=0), (8, 128))
+            column = jnp.where(iota(0) == lane, column, 0.0).sum(axis=1, keepdims=True)
+            side_high[...] = jnp.broadcast_to(column, (8, 128))
+
+        send_totals(4)
+        sent = 2 * (chips - 1) + 2 * (nz - 1)
+        pl.when(me_z == 0)(lambda: wait_all(cells.at[pl.ds(0, sent // tiles)], out_sem))
+        pl.when(me_z > 0)(lambda: wait_all(cells.at[pl.ds(0, (sent + chips // 8) // tiles)], out_sem))
+        wait_totals(7)
         make_top(top_total[1], [top_total[2], top_total[3]], top_halo[...])
-        for send, (out, count) in enumerate(((~last, 3), (chip > 0, 3), (~top, 2), (me_z > 0, 2))):
+        for send, (out, count) in enumerate(((~last, 3), (chip > 0, 3), (~top, 2))):
             pl.when(out)(lambda: wait_all(top_total.at[pl.ds(0, count)], edge_out.at[send]))
+        wait_totals(1, 2)
+        make_side(True)
+        pl.when(~top)(lambda: wait_all(side_high, edge_out.at[3]))
         wait_all(top_part.at[pl.ds(0, 3)], edge_out.at[4])
-        wait_totals(1, 2, 3)
-        make_side(True)
 
 
 def unpack(maps, side_out, top_out):
@@ -310,7 +338,11 @@
                 blocks(chips, 2),
                 blocks(chips, 2),
                 blocks(2),
-                blocks(2, 2),
+                blocks(2),
+                blocks(),
+                blocks(),
+                blocks(chips),
+                blocks(chips),
                 blocks(CHUNKS),
                 blocks(nz, 2),
                 blocks(2 * nz, 2),

time: 17.1 us -> 16.6 us (0.971)
  Pallas kernels: 16.3 us -> 15.9 us
    pallas_call x1, Pallas kernels: 15.7 us -> 15.2 us  [body(): pl.pallas_call(functools.partial(kernel, ny, nz, 1.0 / math.sqrt(depth *...]
where the time goes in v7:
time: 16.6 us; the launch traced here: 16.5 us
  Pallas kernels  15.9 us (96%)
  between operations  0.64 us (4%)
    pallas_call x1, Pallas kernels, body(): pl.pallas_call(functools.partial(kernel, ny, nz, 1.0 / math.sqrt(depth *...  15.2 us
    pallas_call x1, Pallas kernels, body(): pl.pallas_call(unpack, out_shape=(jax.ShapeDtypeStruct((3, rows // ny, wi...  0.62 us

profile of v7, /device:TPU:1, one launch (start us, length us, event | category | flops | bytes accessed | tf_op | source)
XLA Modules:
  0.0 16.5 jit_solution(9811104586552656009)
XLA Ops:
  0.6 15.2 %views.1.maps = f32[12,8,128]{2,1,0:T(8,128)S(1)} custom-call(f32[256,16,256]{2,1,0:T(8,128)} %density.1), custom_call_target="tpu_custom_call" | custom-call | tf_op jit(solution)/shard_map/views/pallas_call | solution.py:330
  15.9 0.6 %unpack.1 = (f32[3,4,256]{2,1,0:T(4,128)}, f32[3,16,64]{2,1,0:T(8,128)}) custom-call(f32[12,8,128]{2,1,0:T(8,128)S(1)} %views.1.maps), custom_call_target="tpu_custom_call" | custom-call | tf_op jit(solution)/shard_map/unpack/pallas_call | solution.py:366

commit v8 on v7

--- a/solution.py
+++ b/solution.py
@@ -53,7 +53,7 @@
         )
 
 
-def kernel(ny, nz, y_factor, z_factor, density, maps_out, cells, side_part, side_mate, side_recv, side_total, side_halo, side_low, side_high, edge_part, edge_recv,
+def kernel(ny, nz, y_factor, z_factor, density, maps_out, cells, side_part, side_mate, side_recv, side_total, side_halo, side_low, side_high, side_next, edge_part, edge_recv,
            top_half, top_part, top_recv, top_total, top_halo, load_sem, chunk_sem, out_sem, side_sem, top_sem, edge_out,
            edge_in, line_sem, ready_sem):
     rows, depth, width = cells.shape
@@ -63,6 +63,9 @@
     me_y, me_z = lax.axis_index("gy"), lax.axis_index("gz")
     chip, core = me_y // 2, me_y % 2
     leads, follows = core == 1, core == 0
+    top = me_z == nz - 1
+    rows_in, rows_out = me_z < nz // 2, (me_z > 0) & (me_z <= nz // 2)
+    next_in, next_out = (me_z >= nz // 2) & ~top, me_z > nz // 2
     lead, mate = (2 * chip + 1, me_z), (2 * chip, me_z)
 
     def load(i):
@@ -85,19 +88,19 @@
 
     barrier = pltpu.get_barrier_semaphore()
 
+    for z in range(1, nz):
+        pl.when(me_z < z)(lambda: signal(barrier, (2 * chip, z)))
+
     @pl.when(leads)
     def _():
         signal(barrier, mate)
         for n in range(chips):
             pl.when(chip != n)(lambda: signal(barrier, (2 * n + 1, me_z)))
 
-        @pl.when(me_z < nz - 1)
+        @pl.when(rows_in)
         def _():
             for n in range(chips):
                 signal(barrier, (2 * n + 1, me_z + 1))
-
-    for z in range(1, nz):
-        pl.when(me_z < z)(lambda: signal(barrier, (2 * chip, z)))
 
     lane = iota(1)
 
@@ -132,7 +135,7 @@
             )
         at = pl.ds(j * owners, owners)
         side_part[at] += side_mate[at]
-        @pl.when(me_z > 0)
+        @pl.when(rows_out)
         def _():
             columns = jnp.broadcast_to(side_part[at, 0][:, :, :1], (owners, 8, 128))
             edge_part[at, 0:1] = jnp.where((iota(0) == lane)[None], columns, 0.0).sum(axis=1, keepdims=True)
@@ -151,7 +154,7 @@
         return carry
 
     def send_top(z):
-        remote(top_part.at[z], top_recv.at[2 * me_z + core], out_sem, top_sem, (2 * chip + 1, z)).start()
+        remote(top_part.at[z], top_recv.at[core * nz + me_z], out_sem, top_sem.at[core], (2 * chip + 1, z)).start()
 
     def pack(z, above):
         here = top_half[2 * z] + top_half[2 * z + 1]
@@ -194,8 +197,8 @@
 
     @pl.when(leads)
     def _():
-        pl.when(me_z == 0)(lambda: pl.semaphore_wait(barrier, chips - 1))
-        pl.when(me_z > 0)(lambda: pl.semaphore_wait(barrier, 2 * chips - 1))
+        pl.when(~rows_out)(lambda: pl.semaphore_wait(barrier, chips - 1))
+        pl.when(rows_out)(lambda: pl.semaphore_wait(barrier, 2 * chips - 1))
         lax.fori_loop(0, 2, send_side, 0)
 
     lax.fori_loop(CHUNKS - 1, CHUNKS, step, 0)
@@ -206,17 +209,21 @@
             pl.when(me_z < z)(lambda: send_top(z))
 
     up, down = 2 * chip + 3, 2 * chip - 1
-    last, top = chip == chips - 1, me_z == nz - 1
+    last = chip == chips - 1
+    first_in, first_out = (chip == 0) & (me_z == 0), (chip == 0) & (me_z == 1)
+    passes = rows_in & ~first_in
     totals = (
         (side_total, side_halo, ~last, chip > 0, (up - 1, me_z), 0, edge_in.at[0]),
         (side_total, side_halo, chip > 0, ~last, (down, me_z), 1, edge_in.at[0]),
         (side_total.at[1], side_low, ~top, me_z > 0, (me_y, me_z + 1), 2, edge_in.at[1]),
         (side_total.at[1], side_low, ~top, me_z > 0, (2 * chip, me_z + 1), 2, edge_in.at[1]),
-        (side_high, side_high, ~top, ~top, mate, 3, edge_in.at[2]),
+        (side_high.at[pl.ds(0, 1)], side_high.at[pl.ds(0, 1)], passes, passes, mate, 3, edge_in.at[2]),
         (side_total, side_total, leads, follows, mate, 4, side_sem),
         (top_total.at[3], top_halo, ~last, chip > 0, (up - 1, me_z), 0, edge_in.at[3]),
         (top_total.at[0], top_halo, chip > 0, ~last, (down, me_z), 1, edge_in.at[3]),
-        (top_total, top_total, leads, follows, mate, 4, top_sem),
+        (top_total, top_total, leads, follows, mate, 4, top_sem.at[0]),
+        (side_total.at[0], side_next, next_out, next_in, (me_y, me_z - 1), 5, edge_in.at[2]),
+        (side_total.at[0], side_next, next_out | first_out, next_in | first_in, (2 * chip, me_z - 1), 5, edge_in.at[2]),
     )
 
     def total(k):
@@ -235,7 +242,7 @@
     def _():
         side_low[...] = nothing
 
-    @pl.when(top)
+    @pl.when(~rows_in)
     def _():
         side_high[...] = nothing
 
@@ -247,7 +254,9 @@
     def make_side(shift):
         beside = [side_halo[h] for h in range(2)]
         parts = [side_total[h] for h in range(2)]
-        for h, maps in enumerate(side_maps(parts, beside, beside, side_low[...], side_high[...], y_factor)):
+        high = jnp.where(iota(0) == lane, jnp.broadcast_to(side_high[0:1], (8, 128)), 0.0).sum(axis=1, keepdims=True)
+        high = jnp.where(next_in if shift else next_in | first_in, side_next[...], jnp.broadcast_to(high, (8, 128)))
+        for h, maps in enumerate(side_maps(parts, beside, beside, side_low[...], high, y_factor)):
             for i in range(3):
                 maps_out[2 * i + h] = pltpu.roll(maps[i], 4, 0) if shift else maps[i]
 
@@ -263,7 +272,7 @@
         send_up()
         wait_totals(8, 6)
         make_top(top_halo[...], [top_total[0], top_total[1]], top_total[2])
-        wait_totals(5, 0, 3, 4)
+        wait_totals(5, 0, 3, 4, 10)
         make_side(False)
         wait_all(cells.at[pl.ds(0, (2 * chips + 2 * nz) // tiles)], out_sem)
 
@@ -273,39 +282,38 @@
         pack(nz - 1, nothing)
         send_up()
         side_recv[chip] = side_part[chip]
-        top_recv[2 * me_z + 1] = top_part[me_z]
+        top_recv[nz + me_z] = top_part[me_z]
 
         wait_all(side_recv.at[pl.ds(0, chips - 1)], side_sem)
         side_total[...] = side_recv[...].sum(axis=0)
-        send_totals(2, 3, 1, 0, 5)
-
-        wait_all(top_recv.at[pl.ds(0, 2 * nz - 1)], top_sem)
-        for h in range(4):
-            added = top_recv[h // 2, h % 2]
-            for z in range(1, nz):
-                added += top_recv[2 * z + h // 2, h % 2]
-            top_total[h] = added
-        send_totals(7, 6, 8)
-
-        @pl.when(~top)
+        send_totals(9, 10, 2, 3, 1, 0, 5)
+
+        wait_all(top_recv.at[pl.ds(0, nz - 1)], top_sem.at[1])
+        top_total[2:4] = top_recv[nz : 2 * nz].sum(axis=0)
+        send_totals(6)
+        wait_all(top_recv.at[pl.ds(0, nz)], top_sem.at[0])
+        top_total[0:2] = top_recv[0:nz].sum(axis=0)
+        send_totals(7, 8)
+
+        @pl.when(rows_in)
         def _():
             wait_all(edge_recv.at[pl.ds(0, chips), pl.ds(0, 1)], edge_in.at[2])
-            column = jnp.broadcast_to(edge_recv[:, 0:1].sum(axis=0), (8, 128))
-            column = jnp.where(iota(0) == lane, column, 0.0).sum(axis=1, keepdims=True)
-            side_high[...] = jnp.broadcast_to(column, (8, 128))
+            side_high[0:1] = edge_recv[:, 0:1].sum(axis=0)
 
         send_totals(4)
         sent = 2 * (chips - 1) + 2 * (nz - 1)
-        pl.when(me_z == 0)(lambda: wait_all(cells.at[pl.ds(0, sent // tiles)], out_sem))
-        pl.when(me_z > 0)(lambda: wait_all(cells.at[pl.ds(0, (sent + chips // 8) // tiles)], out_sem))
+        pl.when(~rows_out)(lambda: wait_all(cells.at[pl.ds(0, sent // tiles)], out_sem))
+        pl.when(rows_out)(lambda: wait_all(cells.at[pl.ds(0, (sent + chips // 8) // tiles)], out_sem))
         wait_totals(7)
         make_top(top_total[1], [top_total[2], top_total[3]], top_halo[...])
         for send, (out, count) in enumerate(((~last, 3), (chip > 0, 3), (~top, 2))):
             pl.when(out)(lambda: wait_all(top_total.at[pl.ds(0, count)], edge_out.at[send]))
-        wait_totals(1, 2)
+        wait_totals(1, 2, 9)
         make_side(True)
-        pl.when(~top)(lambda: wait_all(side_high, edge_out.at[3]))
+        pl.when(passes)(lambda: wait_all(side_high.at[pl.ds(0, 1)], edge_out.at[3]))
         wait_all(top_part.at[pl.ds(0, 3)], edge_out.at[4])
+        pl.when(next_out)(lambda: wait_all(top_total.at[pl.ds(0, 2)], edge_out.at[5]))
+        pl.when(first_out)(lambda: wait_all(side_next, edge_out.at[5]))
 
 
 def unpack(maps, side_out, top_out):
@@ -341,6 +349,7 @@
                 blocks(2),
                 blocks(),
                 blocks(),
+                blocks(),
                 blocks(chips),
                 blocks(chips),
                 blocks(CHUNKS),
@@ -352,8 +361,8 @@
                 pltpu.SemaphoreType.DMA((3,)),
                 pltpu.SemaphoreType.DMA,
                 pltpu.SemaphoreType.DMA,
-                pltpu.SemaphoreType.DMA,
-                pltpu.SemaphoreType.DMA((5,)),
+                pltpu.SemaphoreType.DMA((2,)),
+                pltpu.SemaphoreType.DMA((6,)),
                 pltpu.SemaphoreType.DMA((4,)),
                 pltpu.SemaphoreType.REGULAR,
                 pltpu.SemaphoreType.REGULAR,

time: 16.6 us -> 16.2 us (0.976)
  the two profiles are of different devices: /device:TPU:1 before, /device:TPU:89 now
where the time goes in v8:
time: 16.2 us; the launch traced here: 16.1 us
  Pallas kernels  15.5 us (96%)
  between operations  0.64 us (4%)
    pallas_call x1, Pallas kernels, body(): pl.pallas_call(functools.partial(kernel, ny, nz, 1.0 / math.sqrt(depth *...  14.8 us
    pallas_call x1, Pallas kernels, body(): pl.pallas_call(unpack, out_shape=(jax.ShapeDtypeStruct((3, rows // ny, wi...  0.62 us

profile of v8, /device:TPU:89, one launch (start us, length us, event | category | flops | bytes accessed | tf_op | source)
XLA Modules:
  0.0 16.1 jit_solution(1359786691701826713)
XLA Ops:
  0.6 14.8 %views.1.maps = f32[12,8,128]{2,1,0:T(8,128)S(1)} custom-call(f32[256,16,256]{2,1,0:T(8,128)} %density.1), custom_call_target="tpu_custom_call" | custom-call | tf_op jit(solution)/shard_map/views/pallas_call | solution.py:338
  15.5 0.6 %unpack.1 = (f32[3,4,256]{2,1,0:T(4,128)}, f32[3,16,64]{2,1,0:T(8,128)}) custom-call(f32[12,8,128]{2,1,0:T(8,128)S(1)} %views.1.maps), custom_call_target="tpu_custom_call" | custom-call | tf_op jit(solution)/shard_map/unpack/pallas_call | solution.py:375

commit v9 on v8

--- a/solution.py
+++ b/solution.py
@@ -208,22 +208,23 @@
         for z in range(1, nz):
             pl.when(me_z < z)(lambda: send_top(z))
 
-    up, down = 2 * chip + 3, 2 * chip - 1
+    up, down = ((2 * chip + 2) % ny, me_z), ((2 * chip + ny - 1) % ny, me_z)
+    above, below = (me_z + 1) % nz, (me_z + nz - 1) % nz
     last = chip == chips - 1
     first_in, first_out = (chip == 0) & (me_z == 0), (chip == 0) & (me_z == 1)
     passes = rows_in & ~first_in
     totals = (
-        (side_total, side_halo, ~last, chip > 0, (up - 1, me_z), 0, edge_in.at[0]),
-        (side_total, side_halo, chip > 0, ~last, (down, me_z), 1, edge_in.at[0]),
-        (side_total.at[1], side_low, ~top, me_z > 0, (me_y, me_z + 1), 2, edge_in.at[1]),
-        (side_total.at[1], side_low, ~top, me_z > 0, (2 * chip, me_z + 1), 2, edge_in.at[1]),
+        (side_total, side_halo, ~last, chip > 0, up, 0, edge_in.at[0]),
+        (side_total, side_halo, chip > 0, ~last, down, 1, edge_in.at[0]),
+        (side_total.at[1], side_low, ~top, me_z > 0, (me_y, above), 2, edge_in.at[1]),
+        (side_total.at[1], side_low, ~top, me_z > 0, (2 * chip, above), 2, edge_in.at[1]),
         (side_high.at[pl.ds(0, 1)], side_high.at[pl.ds(0, 1)], passes, passes, mate, 3, edge_in.at[2]),
         (side_total, side_total, leads, follows, mate, 4, side_sem),
-        (top_total.at[3], top_halo, ~last, chip > 0, (up - 1, me_z), 0, edge_in.at[3]),
-        (top_total.at[0], top_halo, chip > 0, ~last, (down, me_z), 1, edge_in.at[3]),
+        (top_total.at[3], top_halo, ~last, chip > 0, up, 0, edge_in.at[3]),
+        (top_total.at[0], top_halo, chip > 0, ~last, down, 1, edge_in.at[3]),
         (top_total, top_total, leads, follows, mate, 4, top_sem.at[0]),
-        (side_total.at[0], side_next, next_out, next_in, (me_y, me_z - 1), 5, edge_in.at[2]),
-        (side_total.at[0], side_next, next_out | first_out, next_in | first_in, (2 * chip, me_z - 1), 5, edge_in.at[2]),
+        (side_total.at[0], side_next, next_out, next_in, (me_y, below), 5, edge_in.at[2]),
+        (side_total.at[0], side_next, next_out | first_out, next_in | first_in, (2 * chip, below), 5, edge_in.at[2]),
     )
 
     def total(k):
@@ -295,6 +296,9 @@
         top_total[0:2] = top_recv[0:nz].sum(axis=0)
         send_totals(7, 8)
 
+        wait_totals(7)
+        make_top(top_total[1], [top_total[2], top_total[3]], top_halo[...])
+
         @pl.when(rows_in)
         def _():
             wait_all(edge_recv.at[pl.ds(0, chips), pl.ds(0, 1)], edge_in.at[2])
@@ -304,8 +308,6 @@
         sent = 2 * (chips - 1) + 2 * (nz - 1)
         pl.when(~rows_out)(lambda: wait_all(cells.at[pl.ds(0, sent // tiles)], out_sem))
         pl.when(rows_out)(lambda: wait_all(cells.at[pl.ds(0, (sent + chips // 8) // tiles)], out_sem))
-        wait_totals(7)
-        make_top(top_total[1], [top_total[2], top_total[3]], top_halo[...])
         for send, (out, count) in enumerate(((~last, 3), (chip > 0, 3), (~top, 2))):
             pl.when(out)(lambda: wait_all(top_total.at[pl.ds(0, count)], edge_out.at[send]))
         wait_totals(1, 2, 9)

time: 16.2 us -> 16.2 us (level)
  no operation moved by 1% of the time
where the time goes in v9:
time: 16.2 us; the launch traced here: 16.1 us
  Pallas kernels  15.5 us (96%)
  between operations  0.64 us (4%)
    pallas_call x1, Pallas kernels, body(): pl.pallas_call(functools.partial(kernel, ny, nz, 1.0 / math.sqrt(depth *...  14.8 us
    pallas_call x1, Pallas kernels, body(): pl.pallas_call(unpack, out_shape=(jax.ShapeDtypeStruct((3, rows // ny, wi...  0.62 us

profile of v9, /device:TPU:89, one launch (start us, length us, event | category | flops | bytes accessed | tf_op | source)
XLA Modules:
  0.0 16.1 jit_solution(9053557657405053931)
XLA Ops:
  0.6 14.8 %views.1.maps = f32[12,8,128]{2,1,0:T(8,128)S(1)} custom-call(f32[256,16,256]{2,1,0:T(8,128)} %density.1), custom_call_target="tpu_custom_call" | custom-call | tf_op jit(solution)/shard_map/views/pallas_call | solution.py:340
  15.5 0.6 %unpack.1 = (f32[3,4,256]{2,1,0:T(4,128)}, f32[3,16,64]{2,1,0:T(8,128)}) custom-call(f32[12,8,128]{2,1,0:T(8,128)S(1)} %views.1.maps), custom_call_target="tpu_custom_call" | custom-call | tf_op jit(solution)/shard_map/unpack/pallas_call | solution.py:377

commit v10 on v9

--- a/solution.py
+++ b/solution.py
@@ -10,7 +10,7 @@
 
 MESH = pl.DeviceIdType.MESH
 CHUNKS = 8
-LOADS = 8
+LOADS = ((0, 1), (1, 2), (3, 2), (5, 3))
 
 
 def iota(axis):
@@ -69,10 +69,11 @@
     lead, mate = (2 * chip + 1, me_z), (2 * chip, me_z)
 
     def load(i):
-        at = pl.ds(i * (rows // LOADS), rows // LOADS)
+        first, count = LOADS[i]
+        at = pl.ds(first * span, count * span)
         return pltpu.make_async_copy(density.at[at], cells.at[at], load_sem.at[i])
 
-    for i in range(LOADS):
+    for i in range(len(LOADS)):
         load(i).start()
 
     def remote(src, dst, send, recv, peer):
@@ -105,7 +106,8 @@
     lane = iota(1)
 
     def add(j):
-        pl.when(j % (CHUNKS // LOADS) == 0)(lambda: load(j // (CHUNKS // LOADS)).wait())
+        for i, (first, _) in enumerate(LOADS):
+            pl.when(j == first)(lambda: load(i).wait())
         block = jnp.zeros((8, 128), jnp.float32)
         place = lane - (j * span) % 64
         for k in range(span // 8):
@@ -199,7 +201,7 @@
     def _():
         pl.when(~rows_out)(lambda: pl.semaphore_wait(barrier, chips - 1))
         pl.when(rows_out)(lambda: pl.semaphore_wait(barrier, 2 * chips - 1))
-        lax.fori_loop(0, 2, send_side, 0)
+        lax.fori_loop(0, 4, send_side, 0)
 
     lax.fori_loop(CHUNKS - 1, CHUNKS, step, 0)
 
@@ -279,7 +281,7 @@
 
     @pl.when(leads)
     def _():
-        lax.fori_loop(2, CHUNKS, send_side, 0)
+        lax.fori_loop(4, CHUNKS, send_side, 0)
         pack(nz - 1, nothing)
         send_up()
         side_recv[chip] = side_part[chip]
@@ -359,7 +361,7 @@
                 blocks(2 * nz, 2),
                 blocks(4),
                 blocks(),
-                pltpu.SemaphoreType.DMA((LOADS,)),
+                pltpu.SemaphoreType.DMA((len(LOADS),)),
                 pltpu.SemaphoreType.DMA((3,)),
                 pltpu.SemaphoreType.DMA,
                 pltpu.SemaphoreType.DMA,

time: 16.2 us -> 16.1 us (level)
  no operation moved by 1% of the time
where the time goes in v10:
time: 16.1 us; the launch traced here: 16 us
  Pallas kernels  15.4 us (96%)
  between operations  0.64 us (4%)
    pallas_call x1, Pallas kernels, body(): pl.pallas_call(functools.partial(kernel, ny, nz, 1.0 / math.sqrt(depth *...  14.8 us
    pallas_call x1, Pallas kernels, body(): pl.pallas_call(unpack, out_shape=(jax.ShapeDtypeStruct((3, rows // ny, wi...  0.62 us

profile of v10, /device:TPU:89, one launch (start us, length us, event | category | flops | bytes accessed | tf_op | source)
XLA Modules:
  0.0 16.0 jit_solution(9075077542710171611)
XLA Ops:
  0.6 14.8 %views.1.maps = f32[12,8,128]{2,1,0:T(8,128)S(1)} custom-call(f32[256,16,256]{2,1,0:T(8,128)} %density.1), custom_call_target="tpu_custom_call" | custom-call | tf_op jit(solution)/shard_map/views/pallas_call | solution.py:342
  15.4 0.6 %unpack.1 = (f32[3,4,256]{2,1,0:T(4,128)}, f32[3,16,64]{2,1,0:T(8,128)}) custom-call(f32[12,8,128]{2,1,0:T(8,128)S(1)} %views.1.maps), custom_call_target="tpu_custom_call" | custom-call | tf_op jit(solution)/shard_map/unpack/pallas_call | solution.py:379

commit v11 on v10

--- a/solution.py
+++ b/solution.py
@@ -289,7 +289,7 @@
 
         wait_all(side_recv.at[pl.ds(0, chips - 1)], side_sem)
         side_total[...] = side_recv[...].sum(axis=0)
-        send_totals(9, 10, 2, 3, 1, 0, 5)
+        send_totals(0, 2, 3, 10, 9, 5, 1)
 
         wait_all(top_recv.at[pl.ds(0, nz - 1)], top_sem.at[1])
         top_total[2:4] = top_recv[nz : 2 * nz].sum(axis=0)

time: 16.1 us -> 16.1 us (level)
  no operation moved by 1% of the time
where the time goes in v11:
time: 16.1 us; the launch traced here: 16 us
  Pallas kernels  15.4 us (96%)
  between operations  0.64 us (4%)
    pallas_call x1, Pallas kernels, body(): pl.pallas_call(functools.partial(kernel, ny, nz, 1.0 / math.sqrt(depth *...  14.8 us
    pallas_call x1, Pallas kernels, body(): pl.pallas_call(unpack, out_shape=(jax.ShapeDtypeStruct((3, rows // ny, wi...  0.62 us

profile of v11, /device:TPU:89, one launch (start us, length us, event | category | flops | bytes accessed | tf_op | source)
XLA Modules:
  0.0 16.0 jit_solution(13459383033764956646)
XLA Ops:
  0.6 14.8 %views.1.maps = f32[12,8,128]{2,1,0:T(8,128)S(1)} custom-call(f32[256,16,256]{2,1,0:T(8,128)} %density.1), custom_call_target="tpu_custom_call" | custom-call | tf_op jit(solution)/shard_map/views/pallas_call | solution.py:342
  15.4 0.6 %unpack.1 = (f32[3,4,256]{2,1,0:T(4,128)}, f32[3,16,64]{2,1,0:T(8,128)}) custom-call(f32[12,8,128]{2,1,0:T(8,128)S(1)} %views.1.maps), custom_call_target="tpu_custom_call" | custom-call | tf_op jit(solution)/shard_map/unpack/pallas_call | solution.py:379
